TPU v7x, 128 devices: a whole 4x4x4 slice. The times are simulated.
128 devices in a mesh: dx: 16 (over y, z), dy: 8 (over x, core).
Axes of the slice: x: 4, y: 4, z: 4, core: 2. Of those that a mesh axis runs over, the one named last changes fastest.
Arguments:
- coarse_states: bfloat16 [2048, 125, 128], P(('dx', 'dy')), may hold values from -50 to 50
- record_target: int32 [2048], P(('dx', 'dy')), may hold values from 0 to 2047, as said below
- cell_matrix: bfloat16 [343, 343], replicated, may hold values from -0.5 to 2.25, as said below
- mass_scale: float32 [192, 96, 24], P('dx', 'dy'), may hold values from 0.6 to 1.2
- potential: float32 [192, 96, 24], P('dx', 'dy'), may hold values from -2 to 1
- filter_window: float32 [2], replicated, may hold values from 1.5 to 30, as said below
Outputs:
- states: float32 [192, 96, 24, 128], P('dx', 'dy')
- gram: float32 [128, 128], replicated
Inputs may be any that keep to these rules, and one draw needn't show every extreme that they name: record_target is a permutation of the 2048 fine cells; each device receives records for exactly its 16 cells; the records of the device with dx index i and dy index j name only cells of the four devices with dx index i + a and dy index j + b (taken modulo the axes' sizes), a and b each 0 or 1, at least one and at most 8 cells of each of the four; the four counts are the same on every device, and one of them is exactly 8 in every draw. `cell_matrix`: symmetric. filter_window[0] < filter_window[1].
All inputs are finite; a program needn't handle non-finite values.
Results may differ from a plain program's by a relative error of at most 0.0038.
Values may be sent and summed in bfloat16 or wider, within the bound.
A program may use at most 64 MiB of HBM per device.

v0:
```python
import functools

import jax
import jax.numpy as jnp
import numpy as np
from jax import lax
from jax.experimental import pallas as pl
from jax.experimental.pallas import tpu as pltpu
from jax.sharding import PartitionSpec as P

ORDER = 6
COARSE_ORDER = 4
CHEB_DEGREE = 3
POINTS = ORDER + 1
COUNT_Z = 4
SLOT = 8
COLUMN = COUNT_Z * SLOT
ROWS = 12
STATES = 128
PAIRS = 4
KDIM = POINTS * SLOT * SLOT
MESH = pl.DeviceIdType.MESH
F32 = jnp.float32
BF16 = jnp.bfloat16


def shifted(block, axis, distance):
    devices = range(lax.axis_size(axis))
    route = [((i - distance) % len(devices), i) for i in devices]
    return lax.ppermute(block, axis, route)


def node_points(degree_value):
    return -np.cos(np.pi * np.arange(degree_value + 1) / degree_value)


def lagrange_table(fine_degree, coarse_degree):
    targets = node_points(fine_degree)
    sources = node_points(coarse_degree)
    matrix = np.ones((fine_degree + 1, coarse_degree + 1))
    for p in range(coarse_degree + 1):
        for m in range(coarse_degree + 1):
            if m != p:
                matrix[:, p] = matrix[:, p] * (targets - sources[m]) / (sources[p] - sources[m])
    owned_rows = matrix[:fine_degree]
    first = owned_rows[:, None, None, :, None, None]
    second = owned_rows[None, :, None, None, :, None]
    third = owned_rows[None, None, :, None, None, :]
    product = first * second * third
    return product.reshape(fine_degree**3, (coarse_degree + 1) ** 3)


def row_in_slot(shape, axis):
    return lax.broadcasted_iota(jnp.int32, shape, axis) % SLOT


def dot_nn(a, b):
    return lax.dot_general(a, b, (((1,), (0,)), ((), ())), preferred_element_type=F32)


def dot_tn(a, b):
    return lax.dot_general(a, b, (((0,), (0,)), ((), ())), preferred_element_type=F32)


def dot_nt(a, b):
    return lax.dot_general(a, b, (((1,), (1,)), ((), ())), preferred_element_type=F32)


def split_two(value):
    high = value.astype(BF16)
    return high, (value - high.astype(F32)).astype(BF16)


def split_three(value):
    high = value.astype(BF16)
    rest = value - high.astype(F32)
    middle = rest.astype(BF16)
    return high, middle, (rest - middle.astype(F32)).astype(BF16)


def factor_rows(work):
    size = STATES
    sub = lax.broadcasted_iota(jnp.int32, (SLOT, size), 0)
    lane = lax.broadcasted_iota(jnp.int32, (SLOT, size), 1)

    def panel(j, carry):
        base = pl.multiple_of(j * SLOT, SLOT)
        left = work[pl.ds(base, SLOT), 0:size]
        right = work[pl.ds(base, SLOT), size : 2 * size]
        turned = pltpu.roll(left, lax.rem(size - base, size), 1)
        columns = [jnp.broadcast_to(turned[:, m : m + 1], (SLOT, size)) for m in range(SLOT)]
        for m in range(SLOT):
            pivot = jnp.broadcast_to(columns[m][m : m + 1, :], (SLOT, size))
            scale = lax.rsqrt(pivot)
            scale = scale * (1.5 - 0.5 * pivot * scale * scale)
            below = sub > m
            at = sub == m
            coef = columns[m] * scale
            row_left = jnp.broadcast_to(left[m : m + 1, :], (SLOT, size)) * scale
            row_right = jnp.broadcast_to(right[m : m + 1, :], (SLOT, size)) * scale
            for n in range(m + 1, SLOT):
                entry = jnp.broadcast_to(columns[n][m : m + 1, :], (SLOT, size)) * scale
                columns[n] = jnp.where(below, columns[n] - coef * entry, columns[n])
            left = jnp.where(below, left - coef * row_left, jnp.where(at, row_left, left))
            right = jnp.where(below, right - coef * row_right, jnp.where(at, row_right, right))
        work[pl.ds(base, SLOT), 0:size] = left
        work[pl.ds(base, SLOT), size : 2 * size] = right
        later = jnp.where(lane >= base + SLOT, left, 0.0)
        l1, l2, l3 = [v.astype(F32) for v in split_three(later)]
        both = jnp.concatenate([left, right], axis=1)
        b1, b2, b3 = [v.astype(F32) for v in split_three(both)]
        lhs = jnp.concatenate([l1, l1, l2, l1, l3, l2], axis=0).astype(BF16)
        rhs = jnp.concatenate([b1, b2, b1, b3, b1, b2], axis=0).astype(BF16)
        work[...] = work[...] - dot_tn(lhs, rhs)
        return carry

    lax.fori_loop(0, size // SLOT, panel, 0)


def filter_kernel(
    size_x,
    size_y,
    node_total,
    window,
    start,
    mass,
    pot,
    matrix,
    filtered,
    inverse_out,
    gram_out,
    block,
    total,
    rhs,
    send_x,
    send_y,
    take_x,
    take_y,
    take_c,
    back_x,
    back_y,
    back_c,
    got_x,
    got_y,
    got_c,
    split,
    partial,
    piece_in,
    ring_in,
    gram_sum,
    work,
    start_sem,
    send_sems,
    recv_sems,
    sum_send,
    sum_recv,
):
    me_x = lax.axis_index("dx")
    me_y = lax.axis_index("dy")

    def at(step_x, step_y):
        return (lax.rem(me_x + step_x + size_x, size_x), lax.rem(me_y + step_y + size_y, size_y))

    partners = [at(0, d) for d in range(1, size_y)] + [at(d, 0) for d in range(1, size_x)]
    partners += [at(1, 1), at(-1, -1)]
    barrier = pltpu.get_barrier_semaphore()
    for partner in partners:
        pl.semaphore_signal(barrier, inc=1, device_id=partner, device_id_type=MESH)
    fetch = pltpu.make_async_copy(start, block.at[0, 0:ROWS, 0:ROWS], start_sem)
    fetch.start()
    block[1] = jnp.zeros(block.shape[1:], F32)
    total[...] = jnp.zeros(total.shape, F32)
    fetch.wait()
    pl.semaphore_wait(barrier, len(partners))

    low = window[0]
    high = window[1]
    center = (low + high) / 2.0
    radius = (high - low) / 2.0

    def remote(index, src, dst, step_x, step_y):
        return pltpu.make_async_remote_copy(
            src_ref=src,
            dst_ref=dst,
            send_sem=send_sems.at[index],
            recv_sem=recv_sems.at[index],
            device_id=at(step_x, step_y),
            device_id_type=MESH,
        )

    def column(q, e, f):
        base_x = e * ORDER
        base_y = f * ORDER
        for a in range(POINTS):
            for i in range(PAIRS):
                for h in range(COUNT_Z):
                    parts = []
                    for b in (2 * i, 2 * i + 1):
                        if b < POINTS:
                            rows = pl.ds(h * SLOT, SLOT)
                            parts.append(
                                mass[base_x + a, base_y + b, rows]
                                * block[q, base_x + a, base_y + b, rows]
                            )
                        else:
                            parts.append(jnp.zeros((SLOT, STATES), F32))
                    rhs[
                        pl.ds((a * PAIRS + i) * 2 * SLOT, 2 * SLOT), pl.ds(h * STATES, STATES)
                    ] = jnp.concatenate(parts, axis=0).astype(BF16)
        product = dot_nn(matrix[...], rhs[...])
        for a in range(POINTS):
            for b in range(POINTS):
                first = (a * SLOT + b) * SLOT
                for h in range(COUNT_Z):
                    rows = pl.ds(h * SLOT, SLOT)
                    total[base_x + a, base_y + b, rows] += product[
                        first : first + SLOT, h * STATES : (h + 1) * STATES
                    ]

    def finish(q, x, y, count, alpha, beta):
        shape = (count, COLUMN, STATES)
        slot_row = row_in_slot(shape, 1)
        ys = pl.ds(y, count)
        raw = total[x, ys]
        total[x, ys] = jnp.zeros(shape, F32)
        summed = raw + jnp.where(slot_row == 0, pltpu.roll(raw, SLOT - ORDER, 1), 0.0)
        again = pltpu.roll(summed, COLUMN - SLOT + ORDER, 1)
        full = jnp.where(slot_row < ORDER, summed, jnp.where(slot_row == ORDER, again, 0.0))
        value = block[q, x, ys]
        result = mass[x, ys] * full + (pot[x, ys] - center) * value
        block[1 - q, x, ys] = alpha * result - beta * block[1 - q, x, ys]

    def one_apply(k, p):
        q = lax.rem(p * CHEB_DEGREE + k, 2)
        first = k == 0
        alpha = jnp.where(first, 1.0, 2.0) / radius
        beta = jnp.where(first, 0.0, 1.0)
        send_x[...] = (mass[0, 0:ROWS] * block[q, 0, 0:ROWS]).astype(BF16)
        send_y[...] = (mass[0:ROWS, 0] * block[q, 0:ROWS, 0]).astype(BF16)
        values = [
            remote(0, send_x, take_x, -1, 0),
            remote(1, send_y, take_y, 0, -1),
            remote(2, send_x.at[0], take_c, -1, -1),
        ]
        for copy in values:
            copy.start()
        column(q, 0, 0)
        for copy in values:
            copy.wait()
        block[q, ROWS, 0:ROWS] = take_x[...].astype(F32)
        block[q, 0:ROWS, ROWS] = take_y[...].astype(F32)
        block[q, ROWS, ROWS] = take_c[...].astype(F32)

        def others(index, carry):
            column(q, index // 2, lax.rem(index, 2))
            return carry

        lax.fori_loop(1, 4, others, 0)
        back_x[...] = total[ROWS, 0:ROWS].astype(BF16)
        back_y[...] = total[0:ROWS, ROWS].astype(BF16)
        back_c[...] = total[ROWS, ROWS].astype(BF16)
        sums = [
            remote(3, back_x, got_x, 1, 0),
            remote(4, back_y, got_y, 0, 1),
            remote(5, back_c, got_c, 1, 1),
        ]
        for copy in sums:
            copy.start()
        total[ROWS] = jnp.zeros(total.shape[1:], F32)
        total[0:ROWS, ROWS] = jnp.zeros((ROWS, COLUMN, STATES), F32)

        def interior(x, carry):
            finish(q, x, 1, ROWS - 1, alpha, beta)
            return carry

        lax.fori_loop(1, ROWS, interior, 0)
        for copy in sums:
            copy.wait()
        total[0, 0:ROWS] += got_x[...].astype(F32)
        total[0:ROWS, 0] += got_y[...].astype(F32)
        total[0, 0] += got_c[...].astype(F32)
        finish(q, 0, 0, ROWS, alpha, beta)

        def edge(x, carry):
            finish(q, x, 0, 1, alpha, beta)
            return carry

        lax.fori_loop(1, ROWS, edge, 0)

    def sum_everywhere(p):
        share = STATES // size_y

        def move(index, src, dst, device):
            return pltpu.make_async_remote_copy(
                src_ref=src,
                dst_ref=dst,
                send_sem=sum_send.at[p, index],
                recv_sem=sum_recv.at[p, index],
                device_id=device,
                device_id_type=MESH,
            )

        def rows_of(owner):
            return pl.ds(pl.multiple_of(owner * share, SLOT), share)

        mine = rows_of(me_y)
        copies = []
        for d in range(1, size_y):
            device = at(0, d)
            copies.append(
                move(d - 1, partial.at[rows_of(device[1])], piece_in.at[p, d - 1], device)
            )
        for copy in copies:
            copy.start()
        for copy in copies:
            copy.wait()
        piece = partial[mine, :]
        for d in range(1, size_y):
            piece = piece + piece_in[p, d - 1]
        ring_in[p, me_x] = piece
        copies = []
        for d in range(1, size_x):
            copies.append(
                move(size_y + d - 2, ring_in.at[p, me_x], ring_in.at[p, me_x], at(d, 0))
            )
        for copy in copies:
            copy.start()
        for copy in copies:
            copy.wait()
        piece = ring_in[p, 0]
        for d in range(1, size_x):
            piece = piece + ring_in[p, d]
        gram_sum[p, mine] = piece / node_total
        copies = []
        for d in range(1, size_y):
            copies.append(
                move(
                    size_y + size_x + d - 3, gram_sum.at[p, mine], gram_sum.at[p, mine], at(0, d)
                )
            )
        for copy in copies:
            copy.start()
        for copy in copies:
            copy.wait()

    def one_pass(p, carry):
        def step(k, inner):
            one_apply(k, p)
            return inner

        lax.fori_loop(0, CHEB_DEGREE, step, 0)
        q = lax.rem((p + 1) * CHEB_DEGREE, 2)

        def divide(x, inner):
            shape = (ROWS, COLUMN, STATES)
            value = jnp.where(row_in_slot(shape, 1) < ORDER, block[q, x, 0:ROWS], 0.0)
            high_part, low_part = split_two(value.reshape(ROWS * COLUMN, STATES))
            rows = pl.ds(pl.multiple_of(x * ROWS * COLUMN, ROWS * COLUMN), ROWS * COLUMN)
            split[rows, 0:STATES] = high_part
            split[rows, STATES : 2 * STATES] = low_part
            return inner

        lax.fori_loop(0, ROWS, divide, 0)
        products = dot_tn(split[:, 0:STATES], split[...])
        cross = products[:, STATES : 2 * STATES]
        partial[...] = products[:, 0:STATES] + cross + cross.T
        sum_everywhere(p)
        whole = gram_sum[p]
        work[:, 0:STATES] = whole
        diagonal = lax.broadcasted_iota(jnp.int32, (STATES, STATES), 0) == lax.broadcasted_iota(
            jnp.int32, (STATES, STATES), 1
        )
        work[:, STATES : 2 * STATES] = jnp.where(diagonal, 1.0, 0.0)
        factor_rows(work)
        inverse = work[:, STATES : 2 * STATES]
        inverse_out[...] = inverse
        gram_out[...] = whole

        @pl.when(p == 0)
        def _():
            pair = stacked_inverse(inverse)

            def turn(x, inner):
                value = block[q, x, 0:ROWS].reshape(ROWS * COLUMN, STATES)
                block[q, x, 0:ROWS] = times_inverse(value, pair).reshape(ROWS, COLUMN, STATES)
                return inner

            lax.fori_loop(0, ROWS, turn, 0)

        return carry

    lax.fori_loop(0, 2, one_pass, 0)
    store = pltpu.make_async_copy(block.at[0, 0:ROWS, 0:ROWS], filtered, start_sem)
    store.start()
    store.wait()


def stacked_inverse(inverse):
    high, low = split_two(inverse)
    return jnp.concatenate(
        [jnp.concatenate([high, high], axis=1), jnp.concatenate([low, low], axis=1)], axis=0
    )


def times_inverse(value, pair):
    high, low = split_two(value)
    both = dot_nt(jnp.concatenate([high, low], axis=1), pair)
    return both[:, 0:STATES] + both[:, STATES : 2 * STATES]


def states_kernel(filtered, inverse, out):
    value = filtered[...].reshape(ROWS * COLUMN, STATES)
    result = times_inverse(value, stacked_inverse(inverse[...])).reshape(ROWS, COLUMN, STATES)
    for h in range(COUNT_Z):
        out[0, :, h * ORDER : (h + 1) * ORDER, :] = result[:, h * SLOT : h * SLOT + ORDER, :]


def with_shared_rows(values):
    shape = values.shape
    cells = values.reshape(shape[:2] + (COUNT_Z, ORDER) + shape[3:])
    following = jnp.roll(cells[:, :, :, :1], -1, axis=2)
    cells = jnp.concatenate([cells, following, jnp.zeros_like(following)], axis=3)
    return cells.reshape(shape[:2] + (COLUMN,) + shape[3:])


def place_records(coarse_states, record_target, rows_x, rows_y, rows_z):
    per_device, coarse_count, state_count = coarse_states.shape
    size_x = lax.axis_size("dx")
    size_y = lax.axis_size("dy")
    capacity = per_device // 2
    interp_table = jnp.asarray(lagrange_table(ORDER, COARSE_ORDER), F32).astype(BF16)
    own_x = lax.axis_index("dx")
    own_y = lax.axis_index("dy")
    target = record_target // per_device
    local_cell = record_target % per_device
    step_x = (target // size_y - own_x) % size_x
    step_y = (target % size_y - own_y) % size_y
    bucket = 2 * step_x + step_y
    onehot = (bucket[:, None] == jnp.arange(4, dtype=jnp.int32)[None, :]).astype(jnp.int32)
    before = jnp.cumsum(onehot, axis=0) - onehot
    slot_rank = jnp.sum(before * onehot, axis=1)
    position = bucket * capacity + slot_rank
    payload = jnp.einsum(
        "on,kns->kos", interp_table, coarse_states, preferred_element_type=F32
    ).astype(BF16)
    record_rows = payload.shape[1]
    buffer = jnp.zeros((4 * capacity, record_rows, state_count), BF16).at[position].set(payload)
    buffer = buffer.reshape(4, capacity, record_rows, state_count)
    labels = (
        jnp.full((4 * capacity,), per_device, jnp.int32)
        .at[position]
        .set(local_cell)
        .reshape(4, capacity)
    )
    from_x, labels_x = shifted((buffer[2], labels[2]), "dx", 1)
    from_y, labels_y = shifted((buffer[1], labels[1]), "dy", 1)
    partway, partway_labels = shifted((buffer[3], labels[3]), "dx", 1)
    from_xy, labels_xy = shifted((partway, partway_labels), "dy", 1)
    arrived = jnp.concatenate([buffer[0], from_x, from_y, from_xy], axis=0)
    arrived_labels = jnp.concatenate([labels[0], labels_x, labels_y, labels_xy], axis=0)
    placed = (
        jnp.zeros((per_device + 1, record_rows, state_count), BF16)
        .at[arrived_labels]
        .set(arrived)[:per_device]
    )
    start_block = placed.reshape(2, 2, COUNT_Z, ORDER, ORDER, ORDER, state_count)
    return start_block.transpose(0, 3, 1, 4, 2, 5, 6).reshape(rows_x, rows_y, rows_z, state_count)


def local(coarse_states, record_target, cell_matrix, mass_scale, potential, filter_window):
    rows_x, rows_y, rows_z = mass_scale.shape
    size_x = lax.axis_size("dx")
    size_y = lax.axis_size("dy")
    node_total = float(rows_x * rows_y * rows_z * size_x * size_y)
    start_block = place_records(coarse_states, record_target, rows_x, rows_y, rows_z)
    start_block = with_shared_rows(start_block).astype(F32)
    mass = jnp.pad(
        with_shared_rows(mass_scale), ((0, 1), (0, 1), (0, 0)), constant_values=1.0
    )
    mass = jnp.broadcast_to(mass[..., None], mass.shape + (STATES,))
    pot = with_shared_rows(potential)
    pot = jnp.broadcast_to(pot[..., None], pot.shape + (STATES,))
    plane = POINTS * POINTS
    spread = jnp.pad(
        cell_matrix.reshape((POINTS,) * 6), ((0, 0), (0, 1), (0, 1), (0, 0), (0, 1), (0, 1))
    ).reshape(KDIM, KDIM)
    padded = (ROWS + 1, ROWS + 1, COLUMN, STATES)
    inside = (ROWS, ROWS, COLUMN, STATES)
    face = (ROWS, COLUMN, STATES)
    line = (COLUMN, STATES)
    share = STATES // size_y
    messages = 2 * size_y + size_x - 3
    vmem = pl.BlockSpec(memory_space=pltpu.VMEM)
    anywhere = pl.BlockSpec(memory_space=pl.ANY)
    filtered, inverse, gram_matrix = pl.pallas_call(
        functools.partial(filter_kernel, size_x, size_y, node_total),
        out_shape=(
            jax.ShapeDtypeStruct(inside, F32),
            jax.ShapeDtypeStruct((STATES, STATES), F32),
            jax.ShapeDtypeStruct((STATES, STATES), F32),
        ),
        in_specs=[pl.BlockSpec(memory_space=pltpu.SMEM), anywhere, vmem, vmem, vmem],
        out_specs=(anywhere, vmem, vmem),
        scratch_shapes=[
            pltpu.VMEM((2,) + padded, F32),
            pltpu.VMEM(padded, F32),
            pltpu.VMEM((KDIM, COUNT_Z * STATES), BF16),
            pltpu.VMEM(face, BF16),
            pltpu.VMEM(face, BF16),
            pltpu.VMEM(face, BF16),
            pltpu.VMEM(face, BF16),
            pltpu.VMEM(line, BF16),
            pltpu.VMEM(face, BF16),
            pltpu.VMEM(face, BF16),
            pltpu.VMEM(line, BF16),
            pltpu.VMEM(face, BF16),
            pltpu.VMEM(face, BF16),
            pltpu.VMEM(line, BF16),
            pltpu.VMEM((ROWS * ROWS * COLUMN, 2 * STATES), BF16),
            pltpu.VMEM((STATES, STATES), F32),
            pltpu.VMEM((2, size_y - 1, share, STATES), F32),
            pltpu.VMEM((2, size_x, share, STATES), F32),
            pltpu.VMEM((2, STATES, STATES), F32),
            pltpu.VMEM((STATES, 2 * STATES), F32),
            pltpu.SemaphoreType.DMA,
            pltpu.SemaphoreType.DMA((6,)),
            pltpu.SemaphoreType.DMA((6,)),
            pltpu.SemaphoreType.DMA((2, messages)),
            pltpu.SemaphoreType.DMA((2, messages)),
        ],
        compiler_params=pltpu.CompilerParams(
            collective_id=0, has_side_effects=True, vmem_limit_bytes=52 * 1024 * 1024
        ),
        cost_estimate=pl.CostEstimate(
            flops=6 * 4 * 2 * KDIM * KDIM * 512, bytes_accessed=10_000_000, transcendentals=0
        ),
        name="filter_twice",
    )(filter_window, start_block, mass, pot, spread)
    states = pl.pallas_call(
        states_kernel,
        out_shape=jax.ShapeDtypeStruct((rows_x, rows_y, rows_z, STATES), F32),
        grid=(rows_x,),
        in_specs=[
            pl.BlockSpec((1, ROWS, COLUMN, STATES), lambda x: (x, 0, 0, 0)),
            pl.BlockSpec((STATES, STATES), lambda x: (0, 0)),
        ],
        out_specs=pl.BlockSpec((1, ROWS, rows_z, STATES), lambda x: (x, 0, 0, 0)),
        name="orthonormal_states",
    )(filtered, inverse)
    return (states, gram_matrix)


def solution(mesh):
    in_specs = (
        P(("dx", "dy"), None, None),
        P(("dx", "dy")),
        P(),
        P("dx", "dy", None),
        P("dx", "dy", None),
        P(),
    )
    out_specs = (P("dx", "dy", None, None), P())
    return jax.shard_map(local, mesh=mesh, in_specs=in_specs, out_specs=out_specs, check_vma=False)
```

profile of v0, /device:TPU:1, one launch (start us, length us, event | category | flops | bytes accessed | tf_op | source)
XLA Modules:
  0.0 210.6 jit_solution(12935027421133176673)
XLA Ops:
  0.6 0.7 and_select_fusion
  1.7 1.2 fusion
  3.2 1.5 scatter_fusion
  4.7 1.1 fusion.12
  5.7 2.5 %collective-permute-start.6 = (bf16[8,216,128]{2,1,0:T(8,128)(2,1)}, bf16[8,216,128]{2,1,0:T(8,128)(2,1)}, u32[]{:S(2)}, u32[]{:S(2)}) collective-permute-start(bf16[8,216,128]{2,1,0:T(8,128)(2,1)} %get-tuple-element.9), channel_id=1, source_target_pairs={{120,0},{0,8},{8,16},{16,24},{24,32},{32,40},{40,48},{48,56},{56,6... | collective-permute-start | bytes 1327112 | tf_op jit(solution)/shard_map/ppermute | solution.py:30
  8.2 2.1 collective-permute-start.5
  10.2 1.6 collective-permute-start.4
  12.5 10.4 %collective-permute-done.6 = bf16[8,216,128]{2,1,0:T(8,128)(2,1)} collective-permute-done((bf16[8,216,128]{2,1,0:T(8,128)(2,1)}, bf16[8,216,128]{2,1,0:T(8,128)(2,1)}, u32[]{:S(2)}, u32[]{:S(2)}) %collective-permute-start.6) | collective-permute-done | bytes 442400 | tf_op jit(solution)/shard_map/ppermute | solution.py:30
  22.9 3.2 %collective-permute-start.7 = (bf16[8,216,128]{2,1,0:T(8,128)(2,1)}, bf16[8,216,128]{2,1,0:T(8,128)(2,1)}, u32[]{:S(2)}, u32[]{:S(2)}) collective-permute-start(bf16[8,216,128]{2,1,0:T(8,128)(2,1)} %collective-permute-done.6), channel_id=1, source_target_pairs={{7,0},{0,1},{1,2},{2,3},{3,4},{4,5},{5,6},{6,7},{15,8},{8,9},{9,10... | collective-permute-start | bytes 1327112 | tf_op jit(solution)/shard_map/ppermute | solution.py:30
  26.4 1.0 copy.31
  28.0 5.5 %reshape.207 = bf16[7,7,7,7,7,7]{5,4,3,2,1,0:T(8,128)(2,1)} reshape(bf16[343,343]{1,0:T(8,128)(2,1)S(1)} %copy-done.3) | data formatting | bytes 470596 | tf_op jit(solution)/shard_map/reshape | solution.py:485
  33.5 6.8 %pad.9 = bf16[7,8,8,7,8,8]{5,4,3,2,1,0:T(8,128)(2,1)} pad(bf16[7,7,7,7,7,7]{5,4,3,2,1,0:T(8,128)(2,1)} %reshape.207, bf16[]{:T(256)} %constant.75.clone.1), padding=0_0x0_1x0_1x0_0x0_1x0_1 | pad | bytes 636708 | tf_op jit(solution)/shard_map/jit(_pad)/pad | solution.py:484
  40.3 7.1 %reshape.208.matrix = bf16[448,448]{1,0:T(8,128)(2,1)S(1)} reshape(bf16[7,8,8,7,8,8]{5,4,3,2,1,0:T(8,128)(2,1)} %pad.9) | data formatting | bytes 802816 | tf_op jit(solution)/shard_map/reshape | solution.py:486
  47.8 1.6 collective-permute-start.3
  49.4 4.4 %collective-permute-done = s32[8]{0:T(128)S(1)} collective-permute-done((s32[8]{0:T(128)S(1)}, s32[8]{0:T(128)S(1)}, u32[]{:S(2)}, u32[]{:S(2)}) %collective-permute-start) | collective-permute-done | bytes 64 | tf_op jit(solution)/shard_map/ppermute | solution.py:30
  53.8 2.4 %pad_maximum_fusion = bf16[32,216,128]{2,1,0:T(8,128)(2,1)} fusion(bf16[8,216,128]{2,1,0:T(8,128)(2,1)} %collective-permute-done.7, bf16[8,216,128]{2,1,0:T(8,128)(2,1)S(1)} %collective-permute-done.5, bf16[8,216,128]{2,1,0:T(8,128)(2,1)S(1)} %collective-permute-done.4, bf16[8,216,128]{2,1,0:T(8,128)(2,1)S(1)} %get-tuple-element.8), kind=kLoop, calls=%fused_computation.3 | loop fusion | flops 2654208 | bytes 3538944 | tf_op jit(solution)/shard_map/concatenate | solution.py:459
  56.4 3.9 %scatter_fusion.1 = bf16[17,216,128]{2,1,0:T(8,128)(2,1)S(1)} fusion(bf16[17,216,128]{2,1,0:T(8,128)(2,1)S(1)} %broadcast_in_dim.32, s32[32]{0:T(128)S(1)} %fusion.9, bf16[32,216,128]{2,1,0:T(8,128)(2,1)} %pad_maximum_fusion), kind=kCustom, calls=%fused_computation.2 | custom fusion | bytes 5308544 | tf_op jit(solution)/shard_map/scatter | solution.py:464
  61.3 2.1 %fusion.1.start = f32[12,12,32,128]{3,2,1,0:T(8,128)} fusion(bf16[12,12,1,1,128]{4,3,2,1,0:T(2,128)(2,1)S(1)} %slice.87, bf16[12,12,3,1,128]{4,3,2,1,0:T(2,128)(2,1)S(1)} %slice.86, bf16[12,12,4,6,128]{4,3,2,1,0:T(8,128)(2,1)S(1)} %copy.28, bf16[8]{0:T(256)(128)(2,1)S(1)} %pad.21.clone), kind=kLoop, calls=%fused_computation.7 | loop fusion | flops 5308416 | bytes 3391504 | tf_op jit(solution)/shard_map/convert_element_type | solution.py:476
  63.4 1.8 broadcast_in_dim.39.pot
  65.3 2.0 broadcast_in_dim.37.mass
  67.3 133.2 %filter_twice.1 = (f32[12,12,32,128]{3,2,1,0:T(8,128)}, f32[128,128]{1,0:T(8,128)S(1)}, f32[128,128]{1,0:T(8,128)S(1)}) custom-call(f32[2]{0:T(128)S(1)} %copy-done.2, f32[12,12,32,128]{3,2,1,0:T(8,128)} %fusion.1.start, f32[13,13,32,128]{3,2,1,0:T(8,128)} %broadcast_in_dim.37.mass, f32[12,12,32,128]{3,2,1,0:T(8,128)} %broadcast_in_dim.39.pot, ...), custom_call_target="tpu_custom_call" | custom-call | flops 4932501504 | bytes 10000000 | tf_op jit(solution)/shard_map/filter_twice/pallas_call | solution.py:495
  200.6 0.6 copy-done.1
  201.2 8.8 %orthonormal_states.1 = f32[12,12,24,128]{3,2,1,0:T(8,128)} custom-call(f32[12,12,32,128]{3,2,1,0:T(8,128)} %get-tuple-element.5.filtered, f32[128,128]{1,0:T(8,128)} %copy-done.1), custom_call_target="tpu_custom_call" | custom-call | tf_op jit(solution)/shard_map/orthonormal_states/pallas_call | solution.py:539
  210.0 0.6 copy.39
  (46 shorter events, 3.5 us)
Async XLA Ops:
  0.6 1.1 copy-start
  4.6 21.6 %copy-start.4 = (f32[12,12,24]{2,1,0:T(8,128)S(1)}, f32[12,12,24]{2,1,0:T(8,128)}, u32[]{:S(2)}) copy-start(f32[12,12,24]{2,1,0:T(8,128)} %param.10) | copy-start | bytes 41476
  5.7 22.3 %copy-start.3 = (bf16[343,343]{1,0:T(8,128)(2,1)S(1)}, bf16[343,343]{1,0:T(8,128)(2,1)}, u32[]{:S(2)}) copy-start(bf16[343,343]{1,0:T(8,128)(2,1)} %param.9) | copy-start | bytes 705898
  5.7 17.2 %collective-permute-start.6 = (bf16[8,216,128]{2,1,0:T(8,128)(2,1)}, bf16[8,216,128]{2,1,0:T(8,128)(2,1)}, u32[]{:S(2)}, u32[]{:S(2)}) collective-permute-start(bf16[8,216,128]{2,1,0:T(8,128)(2,1)} %get-tuple-element.9), channel_id=1, source_target_pairs={{120,0},{0,8},{8,16},{16,24},{24,32},{32,40},{40,48},{48,56},{56,6... | collective-permute-start | bytes 1327112 | tf_op jit(solution)/shard_map/ppermute | solution.py:30
  8.2 45.6 %collective-permute-start.5 = (bf16[8,216,128]{2,1,0:T(8,128)(2,1)}, bf16[8,216,128]{2,1,0:T(8,128)(2,1)S(1)}, u32[]{:S(2)}, u32[]{:S(2)}) collective-permute-start(bf16[8,216,128]{2,1,0:T(8,128)(2,1)} %get-tuple-element.10), channel_id=1, source_target_pairs={{7,0},{0,1},{1,2},{2,3},{3,4},{4,5},{5,6},{6,7},{15,8},{8,9},{9,10... | collective-permute-start | bytes 1327112 | tf_op jit(solution)/shard_map/ppermute | solution.py:30
  10.2 43.6 %collective-permute-start.4 = (bf16[8,216,128]{2,1,0:T(8,128)(2,1)S(1)}, bf16[8,216,128]{2,1,0:T(8,128)(2,1)S(1)}, u32[]{:S(2)}, u32[]{:S(2)}) collective-permute-start(bf16[8,216,128]{2,1,0:T(8,128)(2,1)S(1)} %get-tuple-element.11), channel_id=1, source_target_pairs={{120,0},{0,8},{8,16},{16,24},{24,32},{32,40},{40,48},{48,56},{56,6... | collective-permute-start | bytes 1327112 | tf_op jit(solution)/shard_map/ppermute | solution.py:30
  22.9 30.9 %collective-permute-start.7 = (bf16[8,216,128]{2,1,0:T(8,128)(2,1)}, bf16[8,216,128]{2,1,0:T(8,128)(2,1)}, u32[]{:S(2)}, u32[]{:S(2)}) collective-permute-start(bf16[8,216,128]{2,1,0:T(8,128)(2,1)} %collective-permute-done.6), channel_id=1, source_target_pairs={{7,0},{0,1},{1,2},{2,3},{3,4},{4,5},{5,6},{6,7},{15,8},{8,9},{9,10... | collective-permute-start | bytes 1327112 | tf_op jit(solution)/shard_map/ppermute | solution.py:30
  26.2 21.3 %collective-permute-start.2 = (s32[8]{0:T(128)S(1)}, s32[8]{0:T(128)S(1)}, u32[]{:S(2)}, u32[]{:S(2)}) collective-permute-start(s32[8]{0:T(128)S(1)} %get-tuple-element.15), channel_id=1, source_target_pairs={{120,0},{0,8},{8,16},{16,24},{24,32},{32,40},{40,48},{48,56},{56,6... | collective-permute-start | bytes 104 | tf_op jit(solution)/shard_map/ppermute | solution.py:30
  26.2 21.6 %collective-permute-start.1 = (s32[8]{0:T(128)S(1)}, s32[8]{0:T(128)S(1)}, u32[]{:S(2)}, u32[]{:S(2)}) collective-permute-start(s32[8]{0:T(128)S(1)} %get-tuple-element.16), channel_id=1, source_target_pairs={{7,0},{0,1},{1,2},{2,3},{3,4},{4,5},{5,6},{6,7},{15,8},{8,9},{9,10... | collective-permute-start | bytes 104 | tf_op jit(solution)/shard_map/ppermute | solution.py:30
  47.5 6.2 %collective-permute-start = (s32[8]{0:T(128)S(1)}, s32[8]{0:T(128)S(1)}, u32[]{:S(2)}, u32[]{:S(2)}) collective-permute-start(s32[8]{0:T(128)S(1)} %get-tuple-element.17), channel_id=1, source_target_pairs={{120,0},{0,8},{8,16},{16,24},{24,32},{32,40},{40,48},{48,56},{56,6... | collective-permute-start | bytes 104 | tf_op jit(solution)/shard_map/ppermute | solution.py:30
  47.8 6.0 %collective-permute-start.3 = (s32[8]{0:T(128)S(1)}, s32[8]{0:T(128)S(1)}, u32[]{:S(2)}, u32[]{:S(2)}) collective-permute-start(s32[8]{0:T(128)S(1)} %collective-permute-done.2), channel_id=1, source_target_pairs={{7,0},{0,1},{1,2},{2,3},{3,4},{4,5},{5,6},{6,7},{15,8},{8,9},{9,10... | collective-permute-start | bytes 104 | tf_op jit(solution)/shard_map/ppermute | solution.py:30
  65.3 2.0 copy-start.2
  200.5 0.6 copy-start.1
where the time goes:
time: 211 us
  Pallas kernels  142 us (67%)
  local copies, waits for them, and re-layouts  34.7 us (16%)
  waiting for transfers between devices  14.8 us (7%)
  starting transfers between devices  11.2 us (5%)
  other arithmetic  5.81 us (3%)
    pallas_call x1, Pallas kernels, local(): pl.pallas_call(functools.partial(filter_kernel, size_x, size_y, node_tota...  133 us
    ppermute x8, waiting for transfers between devices, shifted(): return lax.ppermute(block, axis, route)  14.8 us
    ppermute x8, starting transfers between devices, shifted(): return lax.ppermute(block, axis, route)  11.2 us
    pallas_call x1, Pallas kernels, local(): pl.pallas_call(states_kernel, out_shape=jax.ShapeDtypeStruct((rows_x, row...  8.8 us
    reshape x1, local copies, waits for them, and re-layouts, local(): spread = jnp.pad(cell_matrix.reshape((POINTS,) * 6), ((0, 0), (0, 1), (0,...  7.09 us
    pad x1, local copies, waits for them, and re-layouts, local(): jnp.pad(cell_matrix.reshape((POINTS,) * 6), ((0, 0), (0, 1), (0, 1), (0,...  6.8 us
    reshape x1, local copies, waits for them, and re-layouts, local(): cell_matrix.reshape((POINTS,) * 6)  5.48 us
  transfers between devices with their start and end apart: 8, of which 2 were waited for; matrix products, arithmetic and copies ran while one was open for 10% of the time, Pallas kernels for 0%

commit v1 on v0

--- a/solution.py
+++ b/solution.py
@@ -19,15 +19,12 @@
 STATES = 128
 PAIRS = 4
 KDIM = POINTS * SLOT * SLOT
+CELLS = 16
+CAPACITY = CELLS // 2
+COARSE_ROWS = 128
 MESH = pl.DeviceIdType.MESH
 F32 = jnp.float32
 BF16 = jnp.bfloat16
-
-
-def shifted(block, axis, distance):
-    devices = range(lax.axis_size(axis))
-    route = [((i - distance) % len(devices), i) for i in devices]
-    return lax.ppermute(block, axis, route)
 
 
 def node_points(degree_value):
@@ -122,13 +119,21 @@
     size_y,
     node_total,
     window,
-    start,
+    targets,
+    target_tile,
+    coarse,
+    table,
+    node_values,
+    cell_matrix,
+    states_out,
+    gram_out,
     mass,
     pot,
     matrix,
-    filtered,
-    inverse_out,
-    gram_out,
+    slots,
+    arrived,
+    target_in,
+    target_list,
     block,
     total,
     rhs,
@@ -149,7 +154,11 @@
     ring_in,
     gram_sum,
     work,
-    start_sem,
+    target_send,
+    target_recv,
+    list_sems,
+    record_send,
+    record_recv,
     send_sems,
     recv_sems,
     sum_send,
@@ -166,12 +175,108 @@
     barrier = pltpu.get_barrier_semaphore()
     for partner in partners:
         pl.semaphore_signal(barrier, inc=1, device_id=partner, device_id_type=MESH)
-    fetch = pltpu.make_async_copy(start, block.at[0, 0:ROWS, 0:ROWS], start_sem)
-    fetch.start()
+    steps = (None, (0, 1), (1, 0), (1, 1))
+    buckets, ranks = [], []
+    counts = [0, 0, 0, 0]
+    for r in range(CELLS):
+        device = targets[r] // CELLS
+        step_x = lax.rem(device // size_y - me_x + size_x, size_x)
+        step_y = lax.rem(lax.rem(device, size_y) - me_y + size_y, size_y)
+        bucket = 2 * step_x + step_y
+        rank = 0
+        for index in range(4):
+            rank = rank + jnp.where(bucket == index, counts[index], 0)
+            counts[index] = counts[index] + jnp.where(bucket == index, 1, 0)
+        buckets.append(bucket)
+        ranks.append(bucket * CAPACITY + rank)
+
+    def record_of(slot):
+        found = 0
+        for r in range(CELLS):
+            found = found + jnp.where(ranks[r] == slot, r, 0)
+        return jnp.minimum(jnp.maximum(found, 0), CELLS - 1)
+
+    last = COARSE_ROWS - 16
+    for index in range(3):
+        slots[index, :, last:COARSE_ROWS] = jnp.zeros((CAPACITY, 16, STATES), BF16)
+    arrived[0:CAPACITY, last:COARSE_ROWS] = jnp.zeros((CAPACITY, 16, STATES), BF16)
+    coarse_count = coarse.shape[1]
+    pl.semaphore_wait(barrier, len(partners))
+    target_copies, record_copies = {}, {}
+    for index in (3, 2, 1):
+        target_copies[index] = pltpu.make_async_remote_copy(
+            src_ref=target_tile,
+            dst_ref=target_in.at[index - 1],
+            send_sem=target_send.at[index - 1],
+            recv_sem=target_recv.at[index - 1],
+            device_id=at(*steps[index]),
+            device_id_type=MESH,
+        )
+        target_copies[index].start()
+    for index in (3, 2, 1):
+        for k in range(CAPACITY):
+            slots[index - 1, k, 0:coarse_count] = coarse[record_of(index * CAPACITY + k)]
+        record_copies[index] = pltpu.make_async_remote_copy(
+            src_ref=slots.at[index - 1],
+            dst_ref=arrived.at[pl.ds(index * CAPACITY, CAPACITY)],
+            send_sem=record_send.at[index - 1],
+            recv_sem=record_recv.at[index - 1],
+            device_id=at(*steps[index]),
+            device_id_type=MESH,
+        )
+        record_copies[index].start()
+    for k in range(CAPACITY):
+        arrived[k, 0:coarse_count] = coarse[record_of(k)]
+
+    place_nodes(node_values, mass, pot)
+    spread_matrix(cell_matrix, matrix)
     block[1] = jnp.zeros(block.shape[1:], F32)
     total[...] = jnp.zeros(total.shape, F32)
-    fetch.wait()
-    pl.semaphore_wait(barrier, len(partners))
+
+    for index in (3, 2, 1):
+        target_copies[index].wait()
+    lists = [
+        pltpu.make_async_copy(target_in.at[i], target_list.at[i], list_sems.at[i]) for i in range(3)
+    ]
+    for copy in lists:
+        copy.start()
+    for copy in lists:
+        copy.wait()
+    own = me_x * size_y + me_y
+    places = [0] * CELLS
+    for index in range(4):
+        seen = 0
+        for r in range(CELLS):
+            target = targets[r] if index == 0 else target_list[index - 1, 0, r]
+            hit = target // CELLS == own
+            cell = jnp.where(hit, lax.rem(target, CELLS), -1)
+            slot = index * CAPACITY + seen
+            for g in range(CELLS):
+                places[g] = places[g] + jnp.where(cell == g, slot, 0)
+            seen = seen + jnp.where(hit, 1, 0)
+    places = [jnp.minimum(jnp.maximum(p, 0), 4 * CAPACITY - 1) for p in places]
+    for index in (3, 2, 1):
+        record_copies[index].wait()
+    slot_row = row_in_slot((COLUMN, STATES), 0)
+    for e in range(2):
+        for f in range(2):
+            for h in range(COUNT_Z):
+                rhs[0:COARSE_ROWS, h * STATES : (h + 1) * STATES] = arrived[
+                    places[(2 * e + f) * COUNT_Z + h]
+                ]
+            fine = dot_nn(table[...], rhs[0:COARSE_ROWS, :]).astype(BF16).astype(F32)
+            for a in range(ORDER):
+                for b in range(ORDER):
+                    first = (a * ORDER + b) * SLOT
+                    lines = [
+                        fine[first : first + SLOT, h * STATES : (h + 1) * STATES]
+                        for h in range(COUNT_Z)
+                    ]
+                    lines = jnp.concatenate(lines, axis=0)
+                    again = pltpu.roll(lines, COLUMN - SLOT + ORDER, 0)
+                    block[0, e * ORDER + a, f * ORDER + b] = jnp.where(
+                        slot_row == ORDER, again, lines
+                    )
 
     low = window[0]
     high = window[1]
@@ -373,26 +478,36 @@
         work[:, STATES : 2 * STATES] = jnp.where(diagonal, 1.0, 0.0)
         factor_rows(work)
         inverse = work[:, STATES : 2 * STATES]
-        inverse_out[...] = inverse
         gram_out[...] = whole
+        pair = stacked_inverse(inverse)
+
+        def turned(x):
+            value = block[q, x, 0:ROWS].reshape(ROWS * COLUMN, STATES)
+            return times_inverse(value, pair).reshape(ROWS, COLUMN, STATES)
 
         @pl.when(p == 0)
         def _():
-            pair = stacked_inverse(inverse)
-
             def turn(x, inner):
-                value = block[q, x, 0:ROWS].reshape(ROWS * COLUMN, STATES)
-                block[q, x, 0:ROWS] = times_inverse(value, pair).reshape(ROWS, COLUMN, STATES)
+                block[q, x, 0:ROWS] = turned(x)
                 return inner
 
             lax.fori_loop(0, ROWS, turn, 0)
 
+        @pl.when(p == 1)
+        def _():
+            def turn(x, inner):
+                result = turned(x)
+                for h in range(COUNT_Z):
+                    states_out[x, :, h * ORDER : (h + 1) * ORDER, :] = result[
+                        :, h * SLOT : h * SLOT + ORDER, :
+                    ]
+                return inner
+
+            lax.fori_loop(0, ROWS, turn, 0)
+
         return carry
 
     lax.fori_loop(0, 2, one_pass, 0)
-    store = pltpu.make_async_copy(block.at[0, 0:ROWS, 0:ROWS], filtered, start_sem)
-    store.start()
-    store.wait()
 
 
 def stacked_inverse(inverse):
@@ -408,63 +523,55 @@
     return both[:, 0:STATES] + both[:, STATES : 2 * STATES]
 
 
-def states_kernel(filtered, inverse, out):
-    value = filtered[...].reshape(ROWS * COLUMN, STATES)
-    result = times_inverse(value, stacked_inverse(inverse[...])).reshape(ROWS, COLUMN, STATES)
-    for h in range(COUNT_Z):
-        out[0, :, h * ORDER : (h + 1) * ORDER, :] = result[:, h * SLOT : h * SLOT + ORDER, :]
-
-
-def with_shared_rows(values):
-    shape = values.shape
-    cells = values.reshape(shape[:2] + (COUNT_Z, ORDER) + shape[3:])
-    following = jnp.roll(cells[:, :, :, :1], -1, axis=2)
-    cells = jnp.concatenate([cells, following, jnp.zeros_like(following)], axis=3)
-    return cells.reshape(shape[:2] + (COLUMN,) + shape[3:])
-
-
-def place_records(coarse_states, record_target, rows_x, rows_y, rows_z):
-    per_device, coarse_count, state_count = coarse_states.shape
-    size_x = lax.axis_size("dx")
-    size_y = lax.axis_size("dy")
-    capacity = per_device // 2
-    interp_table = jnp.asarray(lagrange_table(ORDER, COARSE_ORDER), F32).astype(BF16)
-    own_x = lax.axis_index("dx")
-    own_y = lax.axis_index("dy")
-    target = record_target // per_device
-    local_cell = record_target % per_device
-    step_x = (target // size_y - own_x) % size_x
-    step_y = (target % size_y - own_y) % size_y
-    bucket = 2 * step_x + step_y
-    onehot = (bucket[:, None] == jnp.arange(4, dtype=jnp.int32)[None, :]).astype(jnp.int32)
-    before = jnp.cumsum(onehot, axis=0) - onehot
-    slot_rank = jnp.sum(before * onehot, axis=1)
-    position = bucket * capacity + slot_rank
-    payload = jnp.einsum(
-        "on,kns->kos", interp_table, coarse_states, preferred_element_type=F32
-    ).astype(BF16)
-    record_rows = payload.shape[1]
-    buffer = jnp.zeros((4 * capacity, record_rows, state_count), BF16).at[position].set(payload)
-    buffer = buffer.reshape(4, capacity, record_rows, state_count)
-    labels = (
-        jnp.full((4 * capacity,), per_device, jnp.int32)
-        .at[position]
-        .set(local_cell)
-        .reshape(4, capacity)
-    )
-    from_x, labels_x = shifted((buffer[2], labels[2]), "dx", 1)
-    from_y, labels_y = shifted((buffer[1], labels[1]), "dy", 1)
-    partway, partway_labels = shifted((buffer[3], labels[3]), "dx", 1)
-    from_xy, labels_xy = shifted((partway, partway_labels), "dy", 1)
-    arrived = jnp.concatenate([buffer[0], from_x, from_y, from_xy], axis=0)
-    arrived_labels = jnp.concatenate([labels[0], labels_x, labels_y, labels_xy], axis=0)
-    placed = (
-        jnp.zeros((per_device + 1, record_rows, state_count), BF16)
-        .at[arrived_labels]
-        .set(arrived)[:per_device]
-    )
-    start_block = placed.reshape(2, 2, COUNT_Z, ORDER, ORDER, ORDER, state_count)
-    return start_block.transpose(0, 3, 1, 4, 2, 5, 6).reshape(rows_x, rows_y, rows_z, state_count)
+def place_nodes(node_values, mass, pot):
+    count_z = COUNT_Z * ORDER
+    width = 3 * count_z
+    row = lax.broadcasted_iota(jnp.int32, (COLUMN, width), 0)
+    lane = lax.broadcasted_iota(jnp.int32, (COLUMN, width), 1)
+    within = row % SLOT
+    source = lax.rem((row // SLOT) * ORDER + within, count_z)
+    pick = jnp.where((lax.rem(lane, count_z) == source) & (within < POINTS), 1.0, 0.0)
+    ones = jnp.ones((width, STATES), BF16)
+    third = lax.broadcasted_iota(jnp.int32, (2 * ROWS, width), 1) // count_z
+
+    def one(x, carry):
+        for base, out in ((0, mass), (ROWS * ROWS, pot)):
+            start = pl.multiple_of(base + 2 * ROWS * x, SLOT)
+            values = node_values[pl.ds(start, 2 * ROWS), :]
+            high, middle, low = [v.astype(F32) for v in split_three(values)]
+            parts = jnp.where(third == 0, high, jnp.where(third == 1, middle, low))
+            spread = [
+                jnp.broadcast_to(parts[y : y + 1, :], (COLUMN, width)) * pick
+                for y in range(2 * ROWS)
+            ]
+            lines = dot_nn(jnp.concatenate(spread, axis=0).astype(BF16), ones)
+            lines = lines.reshape(2, ROWS, COLUMN, STATES)
+            out[2 * x, 0:ROWS] = lines[0]
+            out[2 * x + 1, 0:ROWS] = lines[1]
+        return carry
+
+    lax.fori_loop(0, ROWS // 2, one, 0)
+    mass[ROWS] = jnp.ones(mass.shape[1:], F32)
+    mass[0:ROWS, ROWS] = jnp.ones((ROWS, COLUMN, STATES), F32)
+
+
+def spread_matrix(cell_matrix, matrix):
+    nodes = POINTS**3
+    row = lax.broadcasted_iota(jnp.int32, (KDIM, nodes), 0)
+    col = lax.broadcasted_iota(jnp.int32, (KDIM, nodes), 1)
+    b = (row // SLOT) % SLOT
+    c = row % SLOT
+    source = (row // (SLOT * SLOT)) * POINTS * POINTS + b * POINTS + c
+    pick = jnp.where((col == source) & (b < POINTS) & (c < POINTS), 1.0, 0.0).astype(BF16)
+    half = dot_nn(pick, cell_matrix[...]).astype(BF16)
+    matrix[...] = dot_nt(half, pick).astype(BF16)
+
+
+def padded_table():
+    table = lagrange_table(ORDER, COARSE_ORDER).astype(np.float32)
+    table = table.reshape(ORDER * ORDER, ORDER, -1)
+    table = np.pad(table, ((0, 0), (0, SLOT - ORDER), (0, COARSE_ROWS - table.shape[-1])))
+    return jnp.asarray(table.reshape(-1, COARSE_ROWS), F32).astype(BF16)
 
 
 def local(coarse_states, record_target, cell_matrix, mass_scale, potential, filter_window):
@@ -472,18 +579,10 @@
     size_x = lax.axis_size("dx")
     size_y = lax.axis_size("dy")
     node_total = float(rows_x * rows_y * rows_z * size_x * size_y)
-    start_block = place_records(coarse_states, record_target, rows_x, rows_y, rows_z)
-    start_block = with_shared_rows(start_block).astype(F32)
-    mass = jnp.pad(
-        with_shared_rows(mass_scale), ((0, 1), (0, 1), (0, 0)), constant_values=1.0
-    )
-    mass = jnp.broadcast_to(mass[..., None], mass.shape + (STATES,))
-    pot = with_shared_rows(potential)
-    pot = jnp.broadcast_to(pot[..., None], pot.shape + (STATES,))
-    plane = POINTS * POINTS
-    spread = jnp.pad(
-        cell_matrix.reshape((POINTS,) * 6), ((0, 0), (0, 1), (0, 1), (0, 0), (0, 1), (0, 1))
-    ).reshape(KDIM, KDIM)
+    lines = [v.reshape(rows_x * rows_y, rows_z) for v in (mass_scale, potential)]
+    node_values = jnp.concatenate(lines, axis=0)
+    node_values = jnp.concatenate([node_values] * 3, axis=1)
+    target_tile = jnp.pad(record_target[None, :], ((0, SLOT - 1), (0, STATES - CELLS)))
     padded = (ROWS + 1, ROWS + 1, COLUMN, STATES)
     inside = (ROWS, ROWS, COLUMN, STATES)
     face = (ROWS, COLUMN, STATES)
@@ -491,17 +590,22 @@
     share = STATES // size_y
     messages = 2 * size_y + size_x - 3
     vmem = pl.BlockSpec(memory_space=pltpu.VMEM)
-    anywhere = pl.BlockSpec(memory_space=pl.ANY)
-    filtered, inverse, gram_matrix = pl.pallas_call(
+    return pl.pallas_call(
         functools.partial(filter_kernel, size_x, size_y, node_total),
         out_shape=(
-            jax.ShapeDtypeStruct(inside, F32),
-            jax.ShapeDtypeStruct((STATES, STATES), F32),
+            jax.ShapeDtypeStruct((rows_x, rows_y, rows_z, STATES), F32),
             jax.ShapeDtypeStruct((STATES, STATES), F32),
         ),
-        in_specs=[pl.BlockSpec(memory_space=pltpu.SMEM), anywhere, vmem, vmem, vmem],
-        out_specs=(anywhere, vmem, vmem),
+        in_specs=[pl.BlockSpec(memory_space=pltpu.SMEM)] * 2 + [vmem] * 5,
+        out_specs=(vmem, vmem),
         scratch_shapes=[
+            pltpu.VMEM(padded, F32),
+            pltpu.VMEM(inside, F32),
+            pltpu.VMEM((KDIM, KDIM), BF16),
+            pltpu.VMEM((3, CAPACITY, COARSE_ROWS, STATES), BF16),
+            pltpu.VMEM((4 * CAPACITY, COARSE_ROWS, STATES), BF16),
+            pltpu.VMEM((3, SLOT, STATES), jnp.int32),
+            pltpu.SMEM((3, SLOT, STATES), jnp.int32),
             pltpu.VMEM((2,) + padded, F32),
             pltpu.VMEM(padded, F32),
             pltpu.VMEM((KDIM, COUNT_Z * STATES), BF16),
@@ -522,7 +626,11 @@
             pltpu.VMEM((2, size_x, share, STATES), F32),
             pltpu.VMEM((2, STATES, STATES), F32),
             pltpu.VMEM((STATES, 2 * STATES), F32),
-            pltpu.SemaphoreType.DMA,
+            pltpu.SemaphoreType.DMA((3,)),
+            pltpu.SemaphoreType.DMA((3,)),
+            pltpu.SemaphoreType.DMA((3,)),
+            pltpu.SemaphoreType.DMA((3,)),
+            pltpu.SemaphoreType.DMA((3,)),
             pltpu.SemaphoreType.DMA((6,)),
             pltpu.SemaphoreType.DMA((6,)),
             pltpu.SemaphoreType.DMA((2, messages)),
@@ -535,19 +643,7 @@
             flops=6 * 4 * 2 * KDIM * KDIM * 512, bytes_accessed=10_000_000, transcendentals=0
         ),
         name="filter_twice",
-    )(filter_window, start_block, mass, pot, spread)
-    states = pl.pallas_call(
-        states_kernel,
-        out_shape=jax.ShapeDtypeStruct((rows_x, rows_y, rows_z, STATES), F32),
-        grid=(rows_x,),
-        in_specs=[
-            pl.BlockSpec((1, ROWS, COLUMN, STATES), lambda x: (x, 0, 0, 0)),
-            pl.BlockSpec((STATES, STATES), lambda x: (0, 0)),
-        ],
-        out_specs=pl.BlockSpec((1, ROWS, rows_z, STATES), lambda x: (x, 0, 0, 0)),
-        name="orthonormal_states",
-    )(filtered, inverse)
-    return (states, gram_matrix)
+    )(filter_window, record_target, target_tile, coarse_states, padded_table(), node_values, cell_matrix)
 
 
 def solution(mesh):

time: 211 us -> 164 us (0.78)
  local copies, waits for them, and re-layouts: 34.7 us -> 10.2 us
  waiting for transfers between devices: 14.8 us -> 0 us
  starting transfers between devices: 11.2 us -> 0 us
  Pallas kernels: 142 us -> 153 us
  other arithmetic: 5.81 us -> 0.14 us
    pallas_call x1, Pallas kernels: 133 us -> 153 us  [local(): pl.pallas_call(functools.partial(filter_kernel, size_x, size_y, node_tota...]
    ppermute x8 -> x0, waiting for transfers between devices: 14.8 us -> none  [shifted(): return lax.ppermute(block, axis, route)]
    ppermute x8 -> x0, starting transfers between devices: 11.2 us -> none  [shifted(): return lax.ppermute(block, axis, route)]
    reshape x4 -> x2, local copies, waits for them, and re-layouts: 12.6 us -> 1.8 us  [local(): v.reshape(rows_x * rows_y, rows_z)]
    pallas_call x1 -> x0, Pallas kernels: 8.8 us -> none  [local(): pl.pallas_call(states_kernel, out_shape=jax.ShapeDtypeStruct((rows_x, row...]
    pad x2 -> x1, local copies, waits for them, and re-layouts: 6.81 us -> 0.66 us  [local(): jnp.pad(record_target[None, :], ((0, SLOT - 1), (0, STATES - CELLS)))]
    scatter x3 -> x0, local copies, waits for them, and re-layouts: 5.99 us -> none  [the longest x1 3.9 us: place_records(): placed = jnp.zeros((per_device + 1, record_rows, state_count), BF16).at[a...]
    unnamed x14 -> x11, local copies, waits for them, and re-layouts: 2.61 us -> 7.74 us
  transfers between devices with their start and end apart: 8 -> 0, of which waited for: 2 -> 0; matrix products, arithmetic and copies ran while one was open for 10% -> 0% of each run, Pallas kernels for 0% -> 0%
where the time goes in v1:
time: 164 us
  Pallas kernels  153 us (93%)
  local copies, waits for them, and re-layouts  10.2 us (6%)
    pallas_call x1, Pallas kernels, local(): pl.pallas_call(functools.partial(filter_kernel, size_x, size_y, node_tota...  153 us
    unnamed x11, local copies, waits for them, and re-layouts  7.74 us

profile of v1, /device:TPU:1, one launch (start us, length us, event | category | flops | bytes accessed | tf_op | source)
XLA Modules:
  0.0 163.9 jit_solution(4597731301907978330)
XLA Ops:
  0.6 0.7 pad.4.target_tile
  1.3 0.9 reshape.10
  2.2 0.9 reshape.11
  3.1 0.1 maximum_maximum_fusion.node_values
  3.2 1.2 copy.17.coarse
  4.4 0.0 copy-start
  4.4 0.6 copy-done
  5.1 0.0 copy-start.1
  5.1 0.9 copy-done.1
  6.0 0.0 copy-start.2
  6.0 0.7 copy-done.2
  6.7 0.0 copy-start.3
  6.7 0.9 copy-done.3
  7.6 152.9 %filter_twice.1 = (f32[12,12,24,128]{3,2,1,0:T(8,128)}, f32[128,128]{1,0:T(8,128)S(1)}) custom-call(f32[2]{0:T(128)S(1)} %copy-done.2, s32[16]{0:T(128)S(1)} %copy-done, s32[8,128]{1,0:T(8,128)S(1)} %pad.4.target_tile, bf16[16,125,128]{2,1,0:T(8,128)(2,1)S(1)} %copy.17.coarse, bf16[288,128]{1,0:T(8,128)(2,1)S(1)} %copy-done.3, ...), custom_call_target="tpu_custom_call" | custom-call | flops 4932501504 | bytes 10000000 | tf_op jit(solution)/shard_map/filter_twice/pallas_call | solution.py:593
  160.5 2.8 %copy.20 = f32[12,12,24,128]{3,2,1,0:T(8,128)} copy(f32[12,12,24,128]{3,2,1,0:T(8,128)} %get-tuple-element.4) | data formatting | bytes 3538944
  163.3 0.6 copy.21
Async XLA Ops:
  4.4 0.7 copy-start
  5.1 1.0 copy-start.1
  6.0 0.7 copy-start.2
  6.7 0.9 copy-start.3

commit v2 on v1

--- a/solution.py
+++ b/solution.py
@@ -19,6 +19,7 @@
 STATES = 128
 PAIRS = 4
 KDIM = POINTS * SLOT * SLOT
+FACE = SLOT * SLOT
 CELLS = 16
 CAPACITY = CELLS // 2
 COARSE_ROWS = 128
@@ -130,6 +131,9 @@
     mass,
     pot,
     matrix,
+    from_x,
+    from_y,
+    from_xy,
     slots,
     arrived,
     target_in,
@@ -137,11 +141,11 @@
     block,
     total,
     rhs,
+    rhs_taken,
     send_x,
     send_y,
     take_x,
     take_y,
-    take_c,
     back_x,
     back_y,
     back_c,
@@ -171,7 +175,7 @@
         return (lax.rem(me_x + step_x + size_x, size_x), lax.rem(me_y + step_y + size_y, size_y))
 
     partners = [at(0, d) for d in range(1, size_y)] + [at(d, 0) for d in range(1, size_x)]
-    partners += [at(1, 1), at(-1, -1)]
+    partners += [at(1, 1), at(-1, -1), at(1, -1), at(-1, 1)]
     barrier = pltpu.get_barrier_semaphore()
     for partner in partners:
         pl.semaphore_signal(barrier, inc=1, device_id=partner, device_id_type=MESH)
@@ -229,9 +233,8 @@
         arrived[k, 0:coarse_count] = coarse[record_of(k)]
 
     place_nodes(node_values, mass, pot)
-    spread_matrix(cell_matrix, matrix)
+    spread_matrix(cell_matrix, matrix, from_x, from_y, from_xy)
     block[1] = jnp.zeros(block.shape[1:], F32)
-    total[...] = jnp.zeros(total.shape, F32)
 
     for index in (3, 2, 1):
         target_copies[index].wait()
@@ -283,51 +286,75 @@
     center = (low + high) / 2.0
     radius = (high - low) / 2.0
 
-    def remote(index, src, dst, step_x, step_y):
+    def remote(turn, index, src, dst, step_x, step_y):
         return pltpu.make_async_remote_copy(
             src_ref=src,
             dst_ref=dst,
-            send_sem=send_sems.at[index],
-            recv_sem=recv_sems.at[index],
+            send_sem=send_sems.at[turn, index],
+            recv_sem=recv_sems.at[turn, index],
             device_id=at(step_x, step_y),
             device_id_type=MESH,
         )
 
-    def column(q, e, f):
-        base_x = e * ORDER
-        base_y = f * ORDER
-        for a in range(POINTS):
-            for i in range(PAIRS):
+    zeros = jnp.zeros((SLOT, STATES), F32)
+
+    def pack(first, second):
+        return jnp.concatenate([first, second], axis=0).astype(BF16)
+
+    def add_product(product, e, f, points_x, points_y, written):
+        for a in range(points_x):
+            for b in range(points_y):
+                first = (a * SLOT + b) * SLOT
+                x, y = e * ORDER + a, f * ORDER + b
                 for h in range(COUNT_Z):
-                    parts = []
-                    for b in (2 * i, 2 * i + 1):
-                        if b < POINTS:
-                            rows = pl.ds(h * SLOT, SLOT)
-                            parts.append(
-                                mass[base_x + a, base_y + b, rows]
-                                * block[q, base_x + a, base_y + b, rows]
-                            )
-                        else:
-                            parts.append(jnp.zeros((SLOT, STATES), F32))
-                    rhs[
-                        pl.ds((a * PAIRS + i) * 2 * SLOT, 2 * SLOT), pl.ds(h * STATES, STATES)
-                    ] = jnp.concatenate(parts, axis=0).astype(BF16)
-        product = dot_nn(matrix[...], rhs[...])
-        for a in range(POINTS):
-            for b in range(POINTS):
-                first = (a * SLOT + b) * SLOT
-                for h in range(COUNT_Z):
-                    rows = pl.ds(h * SLOT, SLOT)
-                    total[base_x + a, base_y + b, rows] += product[
-                        first : first + SLOT, h * STATES : (h + 1) * STATES
-                    ]
+                    rows = slice(h * SLOT, (h + 1) * SLOT)
+                    part = product[first : first + SLOT, h * STATES : (h + 1) * STATES]
+                    if (x, y) in written:
+                        part = part + total[x, y, rows]
+                    total[x, y, rows] = part
+                written.add((x, y))
+
+    def column(q, e, f, written):
+        points_x = POINTS if e == 0 else ORDER
+        for a in range(points_x):
+            x = e * ORDER + a
+            for h in range(COUNT_Z):
+                rows = slice(h * SLOT, (h + 1) * SLOT)
+                chunks = []
+                for b in range(POINTS):
+                    y = f * ORDER + b
+                    own = y < ROWS
+                    chunks.append(mass[x, y, rows] * block[q, x, y, rows] if own else zeros)
+                chunks.append(chunks[0] if f == 0 else zeros)
+                for i in range(PAIRS):
+                    tile = pack(chunks[2 * i], chunks[2 * i + 1])
+                    copies = [a, POINTS] if (a == 0 and e == 0) else [a]
+                    for place in copies:
+                        first = (place * PAIRS + i) * 2 * SLOT
+                        rhs[first : first + 2 * SLOT, h * STATES : (h + 1) * STATES] = tile
+        depth = FACE * (SLOT if e == 0 else ORDER)
+        product = dot_nn(matrix[:, 0:depth], rhs[0:depth, :])
+        add_product(product, e, f, POINTS, POINTS, written)
+
+    def taken_column(e, f, factor, upper, lower, points_x, points_y, written):
+        for base, lines in ((0, upper), (FACE, lower)):
+            values = [line.astype(F32) for line in lines]
+            for h in range(COUNT_Z):
+                rows = slice(h * SLOT, (h + 1) * SLOT)
+                chunks = [value[rows] for value in values]
+                chunks += [zeros] * (SLOT - len(chunks))
+                for i in range(PAIRS):
+                    first = base + i * 2 * SLOT
+                    rhs_taken[first : first + 2 * SLOT, h * STATES : (h + 1) * STATES] = pack(
+                        chunks[2 * i], chunks[2 * i + 1]
+                    )
+        add_product(dot_nn(factor[...], rhs_taken[...]), e, f, points_x, points_y, written)
 
     def finish(q, x, y, count, alpha, beta):
         shape = (count, COLUMN, STATES)
         slot_row = row_in_slot(shape, 1)
         ys = pl.ds(y, count)
         raw = total[x, ys]
-        total[x, ys] = jnp.zeros(shape, F32)
         summed = raw + jnp.where(slot_row == 0, pltpu.roll(raw, SLOT - ORDER, 1), 0.0)
         again = pltpu.roll(summed, COLUMN - SLOT + ORDER, 1)
         full = jnp.where(slot_row < ORDER, summed, jnp.where(slot_row == ORDER, again, 0.0))
@@ -342,37 +369,45 @@
         beta = jnp.where(first, 0.0, 1.0)
         send_x[...] = (mass[0, 0:ROWS] * block[q, 0, 0:ROWS]).astype(BF16)
         send_y[...] = (mass[0:ROWS, 0] * block[q, 0:ROWS, 0]).astype(BF16)
+        half = pl.ds(ORDER, ORDER)
         values = [
-            remote(0, send_x, take_x, -1, 0),
-            remote(1, send_y, take_y, 0, -1),
-            remote(2, send_x.at[0], take_c, -1, -1),
+            remote(q, 0, send_x, take_x.at[q, pl.ds(ORDER, ROWS)], -1, 0),
+            remote(q, 1, send_y, take_y.at[q, pl.ds(ORDER, ROWS)], 0, -1),
+            remote(q, 2, send_x.at[half], take_x.at[q, pl.ds(0, ORDER)], -1, 1),
+            remote(q, 3, send_y.at[half], take_y.at[q, pl.ds(0, ORDER)], 1, -1),
+            remote(q, 4, send_x.at[pl.ds(0, 1)], take_x.at[q, pl.ds(ORDER + ROWS, 1)], -1, -1),
         ]
         for copy in values:
             copy.start()
-        column(q, 0, 0)
-        for copy in values:
-            copy.wait()
-        block[q, ROWS, 0:ROWS] = take_x[...].astype(F32)
-        block[q, 0:ROWS, ROWS] = take_y[...].astype(F32)
-        block[q, ROWS, ROWS] = take_c[...].astype(F32)
-
-        def others(index, carry):
-            column(q, index // 2, lax.rem(index, 2))
-            return carry
-
-        lax.fori_loop(1, 4, others, 0)
+        written = set()
+        column(q, 1, 1, written)
+        column(q, 0, 1, written)
+        column(q, 1, 0, written)
         back_x[...] = total[ROWS, 0:ROWS].astype(BF16)
         back_y[...] = total[0:ROWS, ROWS].astype(BF16)
         back_c[...] = total[ROWS, ROWS].astype(BF16)
         sums = [
-            remote(3, back_x, got_x, 1, 0),
-            remote(4, back_y, got_y, 0, 1),
-            remote(5, back_c, got_c, 1, 1),
+            remote(q, 5, back_x, got_x.at[q], 1, 0),
+            remote(q, 6, back_y, got_y.at[q], 0, 1),
+            remote(q, 7, back_c, got_c.at[q], 1, 1),
         ]
         for copy in sums:
             copy.start()
-        total[ROWS] = jnp.zeros(total.shape[1:], F32)
-        total[0:ROWS, ROWS] = jnp.zeros((ROWS, COLUMN, STATES), F32)
+        column(q, 0, 0, written)
+        for copy in values:
+            copy.wait()
+        along_x = [take_x[q, line] for line in range(2 * ORDER + POINTS)]
+        along_y = [take_y[q, line] for line in range(3 * ORDER)]
+        last = 2 * ORDER
+        taken_column(
+            1, 1, from_xy, along_x[last:], along_y[last:], ORDER, ORDER, written
+        )
+        taken_column(
+            1, 0, from_x, along_x[ORDER : last + 1], along_x[0:POINTS], ORDER, POINTS, written
+        )
+        taken_column(
+            0, 1, from_y, along_y[ORDER : last + 1], along_y[0:POINTS], POINTS, ORDER, written
+        )
 
         def interior(x, carry):
             finish(q, x, 1, ROWS - 1, alpha, beta)
@@ -381,9 +416,9 @@
         lax.fori_loop(1, ROWS, interior, 0)
         for copy in sums:
             copy.wait()
-        total[0, 0:ROWS] += got_x[...].astype(F32)
-        total[0:ROWS, 0] += got_y[...].astype(F32)
-        total[0, 0] += got_c[...].astype(F32)
+        total[0, 0:ROWS] += got_x[q].astype(F32)
+        total[0:ROWS, 0] += got_y[q].astype(F32)
+        total[0, 0] += got_c[q].astype(F32)
         finish(q, 0, 0, ROWS, alpha, beta)
 
         def edge(x, carry):
@@ -555,16 +590,61 @@
     mass[0:ROWS, ROWS] = jnp.ones((ROWS, COLUMN, STATES), F32)
 
 
-def spread_matrix(cell_matrix, matrix):
+def spread_matrix(cell_matrix, matrix, from_x, from_y, from_xy):
     nodes = POINTS**3
     row = lax.broadcasted_iota(jnp.int32, (KDIM, nodes), 0)
     col = lax.broadcasted_iota(jnp.int32, (KDIM, nodes), 1)
     b = (row // SLOT) % SLOT
     c = row % SLOT
-    source = (row // (SLOT * SLOT)) * POINTS * POINTS + b * POINTS + c
+    source = (row // FACE) * POINTS * POINTS + b * POINTS + c
     pick = jnp.where((col == source) & (b < POINTS) & (c < POINTS), 1.0, 0.0).astype(BF16)
     half = dot_nn(pick, cell_matrix[...]).astype(BF16)
-    matrix[...] = dot_nt(half, pick).astype(BF16)
+    full = dot_nt(half, pick)
+    width = SLOT * FACE
+    full = jnp.concatenate([full, jnp.zeros((KDIM, FACE), F32)], axis=1)
+    lane = lax.broadcasted_iota(jnp.int32, (FACE, width), 1)
+    at_x = lane // FACE == POINTS
+    at_y = (lane // SLOT) % SLOT == POINTS
+
+    def seen(rows, shift, mask):
+        return jnp.where(mask[0 : rows.shape[0]], pltpu.roll(rows, shift, 1), 0.0)
+
+    last_y = [full[a * FACE + ORDER * SLOT : a * FACE + POINTS * SLOT] for a in range(POINTS)]
+    last_x = full[ORDER * FACE : POINTS * FACE]
+    groups = []
+    for a in range(POINTS):
+        group = full[a * FACE : (a + 1) * FACE]
+        first = group[0:SLOT] + seen(last_y[a], SLOT, at_y & (~at_x))
+        if a == 0:
+            first = first + seen(last_y[ORDER], FACE + SLOT, at_y & at_x)
+        group = jnp.concatenate([first, group[SLOT:]], axis=0)
+        if a == 0:
+            group = group + seen(last_x, FACE, at_x & (~at_y))
+        groups.append(group)
+    matrix[...] = jnp.concatenate(groups, axis=0).astype(BF16)
+
+    row = lax.broadcasted_iota(jnp.int32, (KDIM, FACE), 0)
+    col = lax.broadcasted_iota(jnp.int32, (KDIM, FACE), 1)
+    face_x = jnp.where(row == ORDER * FACE + col, 1.0, 0.0)
+    face_y = jnp.where(row == (col // SLOT) * FACE + ORDER * SLOT + col % SLOT, 1.0, 0.0)
+    faces = jnp.concatenate([face_x, face_y], axis=1).astype(BF16)
+    both = dot_nn(full[:, 0:KDIM].astype(BF16), faces)
+    from_xy[...] = both.astype(BF16)
+    low = lax.broadcasted_iota(jnp.int32, (FACE, 2 * FACE), 1) < FACE
+    groups = []
+    for a in range(POINTS):
+        group = both[a * FACE : (a + 1) * FACE]
+        moved = jnp.concatenate(
+            [group[ORDER * SLOT : POINTS * SLOT], jnp.zeros((FACE - SLOT, 2 * FACE), F32)], axis=0
+        )
+        groups.append(jnp.where(low, group, pltpu.roll(moved, FACE, 1)))
+    from_x[...] = jnp.concatenate(groups, axis=0).astype(BF16)
+    groups = []
+    for a in range(POINTS):
+        group = pltpu.roll(both[a * FACE : (a + 1) * FACE], FACE, 1)
+        moved = both[ORDER * FACE : POINTS * FACE] if a == 0 else jnp.zeros_like(group)
+        groups.append(jnp.where(low, group, moved))
+    from_y[...] = jnp.concatenate(groups, axis=0).astype(BF16)
 
 
 def padded_table():
@@ -601,25 +681,28 @@
         scratch_shapes=[
             pltpu.VMEM(padded, F32),
             pltpu.VMEM(inside, F32),
-            pltpu.VMEM((KDIM, KDIM), BF16),
+            pltpu.VMEM((KDIM, SLOT * FACE), BF16),
+            pltpu.VMEM((KDIM, 2 * FACE), BF16),
+            pltpu.VMEM((KDIM, 2 * FACE), BF16),
+            pltpu.VMEM((KDIM, 2 * FACE), BF16),
             pltpu.VMEM((3, CAPACITY, COARSE_ROWS, STATES), BF16),
             pltpu.VMEM((4 * CAPACITY, COARSE_ROWS, STATES), BF16),
             pltpu.VMEM((3, SLOT, STATES), jnp.int32),
             pltpu.SMEM((3, SLOT, STATES), jnp.int32),
             pltpu.VMEM((2,) + padded, F32),
             pltpu.VMEM(padded, F32),
-            pltpu.VMEM((KDIM, COUNT_Z * STATES), BF16),
+            pltpu.VMEM((SLOT * FACE, COUNT_Z * STATES), BF16),
+            pltpu.VMEM((2 * FACE, COUNT_Z * STATES), BF16),
             pltpu.VMEM(face, BF16),
             pltpu.VMEM(face, BF16),
+            pltpu.VMEM((2, 2 * ORDER + POINTS) + line, BF16),
+            pltpu.VMEM((2, 3 * ORDER) + line, BF16),
             pltpu.VMEM(face, BF16),
             pltpu.VMEM(face, BF16),
             pltpu.VMEM(line, BF16),
-            pltpu.VMEM(face, BF16),
-            pltpu.VMEM(face, BF16),
-            pltpu.VMEM(line, BF16),
-            pltpu.VMEM(face, BF16),
-            pltpu.VMEM(face, BF16),
-            pltpu.VMEM(line, BF16),
+            pltpu.VMEM((2,) + face, BF16),
+            pltpu.VMEM((2,) + face, BF16),
+            pltpu.VMEM((2,) + line, BF16),
             pltpu.VMEM((ROWS * ROWS * COLUMN, 2 * STATES), BF16),
             pltpu.VMEM((STATES, STATES), F32),
             pltpu.VMEM((2, size_y - 1, share, STATES), F32),
@@ -631,8 +714,8 @@
             pltpu.SemaphoreType.DMA((3,)),
             pltpu.SemaphoreType.DMA((3,)),
             pltpu.SemaphoreType.DMA((3,)),
-            pltpu.SemaphoreType.DMA((6,)),
-            pltpu.SemaphoreType.DMA((6,)),
+            pltpu.SemaphoreType.DMA((2, 8)),
+            pltpu.SemaphoreType.DMA((2, 8)),
             pltpu.SemaphoreType.DMA((2, messages)),
             pltpu.SemaphoreType.DMA((2, messages)),
         ],

time: 164 us -> 136 us (0.83)
  Pallas kernels: 153 us -> 124 us
    pallas_call x1, Pallas kernels: 153 us -> 124 us  [local(): pl.pallas_call(functools.partial(filter_kernel, size_x, size_y, node_tota...]
where the time goes in v2:
time: 136 us; the launch traced here: 135 us
  Pallas kernels  124 us (91%)
  local copies, waits for them, and re-layouts  10.2 us (7%)
    pallas_call x1, Pallas kernels, local(): pl.pallas_call(functools.partial(filter_kernel, size_x, size_y, node_tota...  124 us
    unnamed x11, local copies, waits for them, and re-layouts  7.74 us

profile of v2, /device:TPU:1, one launch (start us, length us, event | category | flops | bytes accessed | tf_op | source)
XLA Modules:
  0.0 135.3 jit_solution(5939542112007139100)
XLA Ops:
  0.6 0.7 pad.4.target_tile
  1.3 0.9 reshape.10
  2.2 0.9 reshape.11
  3.1 0.1 maximum_maximum_fusion.node_values
  3.2 1.2 copy.17.coarse
  4.4 0.0 copy-start
  4.4 0.6 copy-done
  5.1 0.0 copy-start.1
  5.1 0.9 copy-done.1
  6.0 0.0 copy-start.2
  6.0 0.7 copy-done.2
  6.7 0.0 copy-start.3
  6.7 0.9 copy-done.3
  7.6 124.3 %filter_twice.1 = (f32[12,12,24,128]{3,2,1,0:T(8,128)}, f32[128,128]{1,0:T(8,128)S(1)}) custom-call(f32[2]{0:T(128)S(1)} %copy-done.2, s32[16]{0:T(128)S(1)} %copy-done, s32[8,128]{1,0:T(8,128)S(1)} %pad.4.target_tile, bf16[16,125,128]{2,1,0:T(8,128)(2,1)S(1)} %copy.17.coarse, bf16[288,128]{1,0:T(8,128)(2,1)S(1)} %copy-done.3, ...), custom_call_target="tpu_custom_call" | custom-call | flops 4932501504 | bytes 10000000 | tf_op jit(solution)/shard_map/filter_twice/pallas_call | solution.py:673
  131.9 2.8 %copy.20 = f32[12,12,24,128]{3,2,1,0:T(8,128)} copy(f32[12,12,24,128]{3,2,1,0:T(8,128)} %get-tuple-element.4) | data formatting | bytes 3538944
  134.7 0.6 copy.21
Async XLA Ops:
  4.4 0.7 copy-start
  5.1 1.0 copy-start.1
  6.0 0.7 copy-start.2
  6.7 0.9 copy-start.3

commit v3 on v2

--- a/solution.py
+++ b/solution.py
@@ -20,6 +20,9 @@
 PAIRS = 4
 KDIM = POINTS * SLOT * SLOT
 FACE = SLOT * SLOT
+DEPTH = COUNT_Z * ORDER
+PAIR = 2 * DEPTH
+LINES = ROWS // 2
 CELLS = 16
 CAPACITY = CELLS // 2
 COARSE_ROWS = 128
@@ -121,19 +124,24 @@
     node_total,
     window,
     targets,
-    target_tile,
     coarse,
     table,
-    node_values,
+    mass_in,
+    pot_in,
     cell_matrix,
-    states_out,
+    filtered_out,
+    inverse_out,
     gram_out,
     mass,
     pot,
     matrix,
     from_x,
     from_y,
-    from_xy,
+    shrink,
+    grow,
+    grow_own,
+    target_tile,
+    filtered,
     slots,
     arrived,
     target_in,
@@ -163,6 +171,7 @@
     list_sems,
     record_send,
     record_recv,
+    store_sem,
     send_sems,
     recv_sems,
     sum_send,
@@ -205,6 +214,11 @@
         slots[index, :, last:COARSE_ROWS] = jnp.zeros((CAPACITY, 16, STATES), BF16)
     arrived[0:CAPACITY, last:COARSE_ROWS] = jnp.zeros((CAPACITY, 16, STATES), BF16)
     coarse_count = coarse.shape[1]
+    tile_lane = lax.broadcasted_iota(jnp.int32, (SLOT, STATES), 1)
+    tile = jnp.zeros((SLOT, STATES), jnp.int32)
+    for r in range(CELLS):
+        tile = jnp.where(tile_lane == r, targets[r], tile)
+    target_tile[...] = tile
     pl.semaphore_wait(barrier, len(partners))
     target_copies, record_copies = {}, {}
     for index in (3, 2, 1):
@@ -232,8 +246,9 @@
     for k in range(CAPACITY):
         arrived[k, 0:coarse_count] = coarse[record_of(k)]
 
-    place_nodes(node_values, mass, pot)
-    spread_matrix(cell_matrix, matrix, from_x, from_y, from_xy)
+    place_nodes(mass_in, pot_in, mass, pot)
+    spread_matrix(cell_matrix, matrix, from_x, from_y)
+    line_tables(shrink, grow, grow_own)
     block[1] = jnp.zeros(block.shape[1:], F32)
 
     for index in (3, 2, 1):
@@ -336,26 +351,50 @@
         product = dot_nn(matrix[:, 0:depth], rhs[0:depth, :])
         add_product(product, e, f, POINTS, POINTS, written)
 
-    def taken_column(e, f, factor, upper, lower, points_x, points_y, written):
-        for base, lines in ((0, upper), (FACE, lower)):
-            values = [line.astype(F32) for line in lines]
+    def taken_rows(base, lines, h):
+        chunks = [line[h * SLOT : (h + 1) * SLOT] if line is not None else zeros for line in lines]
+        for i in range(PAIRS):
+            first = base + i * 2 * SLOT
+            rhs_taken[first : first + 2 * SLOT, h * STATES : (h + 1) * STATES] = pack(
+                chunks[2 * i], chunks[2 * i + 1]
+            )
+
+    def taken_column(e, f, factor, runs, points_x, points_y, written):
+        for index, lines in enumerate(runs):
             for h in range(COUNT_Z):
-                rows = slice(h * SLOT, (h + 1) * SLOT)
-                chunks = [value[rows] for value in values]
-                chunks += [zeros] * (SLOT - len(chunks))
-                for i in range(PAIRS):
-                    first = base + i * 2 * SLOT
-                    rhs_taken[first : first + 2 * SLOT, h * STATES : (h + 1) * STATES] = pack(
-                        chunks[2 * i], chunks[2 * i + 1]
-                    )
-        add_product(dot_nn(factor[...], rhs_taken[...]), e, f, points_x, points_y, written)
+                taken_rows(index * FACE, lines, h)
+        depth = FACE * len(runs)
+        product = dot_nn(factor[:, 0:depth], rhs_taken[0:depth, :])
+        add_product(product, e, f, points_x, points_y, written)
+
+    def narrow(lines, out):
+        wide = lines.astype(BF16).reshape(LINES, 2 * COLUMN, STATES)
+        wide = jnp.concatenate([wide[i] for i in range(LINES)], axis=1)
+        packed = dot_nn(shrink[...], wide).astype(BF16)
+        for i in range(LINES):
+            out[i] = packed[:, i * STATES : (i + 1) * STATES]
+
+    def widen(pairs, rows_of_slot):
+        wide = dot_nn(rows_of_slot[...], jnp.concatenate(pairs, axis=1))
+        lines = []
+        for i in range(len(pairs)):
+            for half in range(2):
+                lines.append(
+                    wide[half * COLUMN : (half + 1) * COLUMN, i * STATES : (i + 1) * STATES]
+                )
+        return lines
+
+    def folded(raw):
+        axis = raw.ndim - 2
+        first = row_in_slot(raw.shape, axis) == 0
+        return raw + jnp.where(first, pltpu.roll(raw, SLOT - ORDER, axis), 0.0)
 
     def finish(q, x, y, count, alpha, beta):
         shape = (count, COLUMN, STATES)
         slot_row = row_in_slot(shape, 1)
         ys = pl.ds(y, count)
         raw = total[x, ys]
-        summed = raw + jnp.where(slot_row == 0, pltpu.roll(raw, SLOT - ORDER, 1), 0.0)
+        summed = folded(raw)
         again = pltpu.roll(summed, COLUMN - SLOT + ORDER, 1)
         full = jnp.where(slot_row < ORDER, summed, jnp.where(slot_row == ORDER, again, 0.0))
         value = block[q, x, ys]
@@ -367,46 +406,56 @@
         first = k == 0
         alpha = jnp.where(first, 1.0, 2.0) / radius
         beta = jnp.where(first, 0.0, 1.0)
-        send_x[...] = (mass[0, 0:ROWS] * block[q, 0, 0:ROWS]).astype(BF16)
-        send_y[...] = (mass[0:ROWS, 0] * block[q, 0:ROWS, 0]).astype(BF16)
-        half = pl.ds(ORDER, ORDER)
-        values = [
-            remote(q, 0, send_x, take_x.at[q, pl.ds(ORDER, ROWS)], -1, 0),
-            remote(q, 1, send_y, take_y.at[q, pl.ds(ORDER, ROWS)], 0, -1),
-            remote(q, 2, send_x.at[half], take_x.at[q, pl.ds(0, ORDER)], -1, 1),
-            remote(q, 3, send_y.at[half], take_y.at[q, pl.ds(0, ORDER)], 1, -1),
-            remote(q, 4, send_x.at[pl.ds(0, 1)], take_x.at[q, pl.ds(ORDER + ROWS, 1)], -1, -1),
+        half = pl.ds(LINES // 2, LINES // 2)
+        quarter = LINES // 2
+        values_x = [
+            remote(q, 0, send_x, take_x.at[q, pl.ds(quarter, LINES)], -1, 0),
+            remote(q, 2, send_x.at[half], take_x.at[q, pl.ds(0, quarter)], -1, 1),
+            remote(
+                q, 3, send_x.at[pl.ds(0, 1)], take_x.at[q, pl.ds(quarter + LINES, 1)], -1, -1
+            ),
         ]
-        for copy in values:
+        value_y = remote(q, 1, send_y, take_y.at[q], 0, -1)
+        sum_x = remote(q, 4, back_x, got_x.at[q], 1, 0)
+        sum_y = remote(q, 5, back_y, got_y.at[q], 0, 1)
+        sum_c = remote(q, 6, back_c, got_c.at[q], 1, 1)
+        narrow(mass[0, 0:ROWS] * block[q, 0, 0:ROWS], send_x)
+        for copy in values_x:
             copy.start()
+        narrow(mass[0:ROWS, 0] * block[q, 0:ROWS, 0], send_y)
+        value_y.start()
         written = set()
         column(q, 1, 1, written)
+        column(q, 1, 0, written)
         column(q, 0, 1, written)
-        column(q, 1, 0, written)
-        back_x[...] = total[ROWS, 0:ROWS].astype(BF16)
-        back_y[...] = total[0:ROWS, ROWS].astype(BF16)
+        narrow(folded(total[0:ROWS, ROWS]), back_y)
+        sum_y.start()
         back_c[...] = total[ROWS, ROWS].astype(BF16)
-        sums = [
-            remote(q, 5, back_x, got_x.at[q], 1, 0),
-            remote(q, 6, back_y, got_y.at[q], 0, 1),
-            remote(q, 7, back_c, got_c.at[q], 1, 1),
-        ]
-        for copy in sums:
-            copy.start()
+        sum_c.start()
+        value_y.wait()
+        along_y = widen([take_y[q, i] for i in range(LINES)], grow)
+        taken_column(1, 1, from_y, [along_y[ORDER:] + [None] * 2], POINTS, ORDER, written)
+        narrow(folded(total[ROWS, 0:ROWS]), back_x)
+        sum_x.start()
+        taken_column(
+            0, 1, from_y, [along_y[0:POINTS] + [along_y[0]]], POINTS, ORDER, written
+        )
         column(q, 0, 0, written)
-        for copy in values:
+        for copy in values_x:
             copy.wait()
-        along_x = [take_x[q, line] for line in range(2 * ORDER + POINTS)]
-        along_y = [take_y[q, line] for line in range(3 * ORDER)]
+        along_x = widen([take_x[q, i] for i in range(quarter + LINES + 1)], grow)
         last = 2 * ORDER
         taken_column(
-            1, 1, from_xy, along_x[last:], along_y[last:], ORDER, ORDER, written
+            1, 1, from_x, [along_x[last : last + POINTS] + [None]], ORDER, ORDER, written
         )
         taken_column(
-            1, 0, from_x, along_x[ORDER : last + 1], along_x[0:POINTS], ORDER, POINTS, written
-        )
-        taken_column(
-            0, 1, from_y, along_y[ORDER : last + 1], along_y[0:POINTS], POINTS, ORDER, written
+            1,
+            0,
+            from_x,
+            [along_x[ORDER : last + 1] + [None], along_x[0:POINTS] + [None]],
+            ORDER,
+            POINTS,
+            written,
         )
 
         def interior(x, carry):
@@ -414,11 +463,13 @@
             return carry
 
         lax.fori_loop(1, ROWS, interior, 0)
-        for copy in sums:
+        for copy in (sum_c, sum_y, sum_x):
             copy.wait()
-        total[0, 0:ROWS] += got_x[q].astype(F32)
-        total[0:ROWS, 0] += got_y[q].astype(F32)
         total[0, 0] += got_c[q].astype(F32)
+        for x, line in enumerate(widen([got_y[q, i] for i in range(LINES)], grow_own)):
+            total[x, 0] += line
+        for y, line in enumerate(widen([got_x[q, i] for i in range(LINES)], grow_own)):
+            total[0, y] += line
         finish(q, 0, 0, ROWS, alpha, beta)
 
         def edge(x, carry):
@@ -492,15 +543,27 @@
         q = lax.rem((p + 1) * CHEB_DEGREE, 2)
 
         def divide(x, inner):
-            shape = (ROWS, COLUMN, STATES)
-            value = jnp.where(row_in_slot(shape, 1) < ORDER, block[q, x, 0:ROWS], 0.0)
-            high_part, low_part = split_two(value.reshape(ROWS * COLUMN, STATES))
-            rows = pl.ds(pl.multiple_of(x * ROWS * COLUMN, ROWS * COLUMN), ROWS * COLUMN)
+            value = block[q, x, 0:ROWS]
+            value = jnp.concatenate(
+                [value[:, h * SLOT : h * SLOT + ORDER] for h in range(COUNT_Z)], axis=1
+            )
+
+            @pl.when(p == 1)
+            def _():
+                filtered[x] = value
+
+            high_part, low_part = split_two(value.reshape(ROWS * DEPTH, STATES))
+            rows = pl.ds(pl.multiple_of(x * ROWS * DEPTH, ROWS * DEPTH), ROWS * DEPTH)
             split[rows, 0:STATES] = high_part
             split[rows, STATES : 2 * STATES] = low_part
             return inner
 
         lax.fori_loop(0, ROWS, divide, 0)
+
+        @pl.when(p == 1)
+        def _():
+            pltpu.make_async_copy(filtered, filtered_out, store_sem).start()
+
         products = dot_tn(split[:, 0:STATES], split[...])
         cross = products[:, STATES : 2 * STATES]
         partial[...] = products[:, 0:STATES] + cross + cross.T
@@ -514,35 +577,23 @@
         factor_rows(work)
         inverse = work[:, STATES : 2 * STATES]
         gram_out[...] = whole
-        pair = stacked_inverse(inverse)
-
-        def turned(x):
-            value = block[q, x, 0:ROWS].reshape(ROWS * COLUMN, STATES)
-            return times_inverse(value, pair).reshape(ROWS, COLUMN, STATES)
+        inverse_out[...] = inverse
 
         @pl.when(p == 0)
         def _():
+            pair = stacked_inverse(inverse)
+
             def turn(x, inner):
-                block[q, x, 0:ROWS] = turned(x)
+                value = block[q, x, 0:ROWS].reshape(ROWS * COLUMN, STATES)
+                block[q, x, 0:ROWS] = times_inverse(value, pair).reshape(ROWS, COLUMN, STATES)
                 return inner
 
             lax.fori_loop(0, ROWS, turn, 0)
 
-        @pl.when(p == 1)
-        def _():
-            def turn(x, inner):
-                result = turned(x)
-                for h in range(COUNT_Z):
-                    states_out[x, :, h * ORDER : (h + 1) * ORDER, :] = result[
-                        :, h * SLOT : h * SLOT + ORDER, :
-                    ]
-                return inner
-
-            lax.fori_loop(0, ROWS, turn, 0)
-
         return carry
 
     lax.fori_loop(0, 2, one_pass, 0)
+    pltpu.make_async_copy(filtered, filtered_out, store_sem).wait()
 
 
 def stacked_inverse(inverse):
@@ -558,39 +609,47 @@
     return both[:, 0:STATES] + both[:, STATES : 2 * STATES]
 
 
-def place_nodes(node_values, mass, pot):
-    count_z = COUNT_Z * ORDER
-    width = 3 * count_z
+def place_nodes(mass_in, pot_in, mass, pot):
+    width = 3 * DEPTH
     row = lax.broadcasted_iota(jnp.int32, (COLUMN, width), 0)
     lane = lax.broadcasted_iota(jnp.int32, (COLUMN, width), 1)
     within = row % SLOT
-    source = lax.rem((row // SLOT) * ORDER + within, count_z)
-    pick = jnp.where((lax.rem(lane, count_z) == source) & (within < POINTS), 1.0, 0.0)
+    source = lax.rem((row // SLOT) * ORDER + within, DEPTH)
+    pick = jnp.where((lax.rem(lane, DEPTH) == source) & (within < POINTS), 1.0, 0.0)
     ones = jnp.ones((width, STATES), BF16)
-    third = lax.broadcasted_iota(jnp.int32, (2 * ROWS, width), 1) // count_z
 
     def one(x, carry):
-        for base, out in ((0, mass), (ROWS * ROWS, pot)):
-            start = pl.multiple_of(base + 2 * ROWS * x, SLOT)
-            values = node_values[pl.ds(start, 2 * ROWS), :]
-            high, middle, low = [v.astype(F32) for v in split_three(values)]
-            parts = jnp.where(third == 0, high, jnp.where(third == 1, middle, low))
+        for values, out in ((mass_in, mass), (pot_in, pot)):
+            parts = [v.astype(F32) for v in split_three(values[x])]
+            parts = jnp.concatenate(parts, axis=1)
             spread = [
-                jnp.broadcast_to(parts[y : y + 1, :], (COLUMN, width)) * pick
-                for y in range(2 * ROWS)
+                jnp.broadcast_to(parts[y : y + 1, :], (COLUMN, width)) * pick for y in range(ROWS)
             ]
             lines = dot_nn(jnp.concatenate(spread, axis=0).astype(BF16), ones)
-            lines = lines.reshape(2, ROWS, COLUMN, STATES)
-            out[2 * x, 0:ROWS] = lines[0]
-            out[2 * x + 1, 0:ROWS] = lines[1]
+            out[x, 0:ROWS] = lines.reshape(ROWS, COLUMN, STATES)
         return carry
 
-    lax.fori_loop(0, ROWS // 2, one, 0)
+    lax.fori_loop(0, ROWS, one, 0)
     mass[ROWS] = jnp.ones(mass.shape[1:], F32)
     mass[0:ROWS, ROWS] = jnp.ones((ROWS, COLUMN, STATES), F32)
 
 
-def spread_matrix(cell_matrix, matrix, from_x, from_y, from_xy):
+def line_tables(shrink, grow, grow_own):
+    row = lax.broadcasted_iota(jnp.int32, (PAIR, 2 * COLUMN), 0)
+    col = lax.broadcasted_iota(jnp.int32, (PAIR, 2 * COLUMN), 1)
+    z = row % DEPTH
+    chosen = (row // DEPTH) * COLUMN + (z // ORDER) * SLOT + z % ORDER
+    shrink[...] = jnp.where(col == chosen, 1.0, 0.0).astype(BF16)
+    row = lax.broadcasted_iota(jnp.int32, (2 * COLUMN, PAIR), 0)
+    col = lax.broadcasted_iota(jnp.int32, (2 * COLUMN, PAIR), 1)
+    c = row % SLOT
+    z = (((row // SLOT) % COUNT_Z) * ORDER + c) % DEPTH
+    same = col == (row // COLUMN) * DEPTH + z
+    grow[...] = jnp.where(same & (c < POINTS), 1.0, 0.0).astype(BF16)
+    grow_own[...] = jnp.where(same & (c < ORDER), 1.0, 0.0).astype(BF16)
+
+
+def spread_matrix(cell_matrix, matrix, from_x, from_y):
     nodes = POINTS**3
     row = lax.broadcasted_iota(jnp.int32, (KDIM, nodes), 0)
     col = lax.broadcasted_iota(jnp.int32, (KDIM, nodes), 1)
@@ -629,7 +688,6 @@
     face_y = jnp.where(row == (col // SLOT) * FACE + ORDER * SLOT + col % SLOT, 1.0, 0.0)
     faces = jnp.concatenate([face_x, face_y], axis=1).astype(BF16)
     both = dot_nn(full[:, 0:KDIM].astype(BF16), faces)
-    from_xy[...] = both.astype(BF16)
     low = lax.broadcasted_iota(jnp.int32, (FACE, 2 * FACE), 1) < FACE
     groups = []
     for a in range(POINTS):
@@ -639,12 +697,11 @@
         )
         groups.append(jnp.where(low, group, pltpu.roll(moved, FACE, 1)))
     from_x[...] = jnp.concatenate(groups, axis=0).astype(BF16)
-    groups = []
-    for a in range(POINTS):
-        group = pltpu.roll(both[a * FACE : (a + 1) * FACE], FACE, 1)
-        moved = both[ORDER * FACE : POINTS * FACE] if a == 0 else jnp.zeros_like(group)
-        groups.append(jnp.where(low, group, moved))
-    from_y[...] = jnp.concatenate(groups, axis=0).astype(BF16)
+    faces_y = pltpu.roll(both, FACE, 1)[:, 0:FACE]
+    seen_y = pltpu.roll(both[ORDER * FACE : POINTS * FACE], FACE + SLOT, 1)[:, 0:FACE]
+    at_end = lax.broadcasted_iota(jnp.int32, (FACE, FACE), 1) >= POINTS * SLOT
+    first = jnp.where(at_end, seen_y, faces_y[0:FACE])
+    from_y[...] = jnp.concatenate([first, faces_y[FACE:]], axis=0).astype(BF16)
 
 
 def padded_table():
@@ -659,32 +716,34 @@
     size_x = lax.axis_size("dx")
     size_y = lax.axis_size("dy")
     node_total = float(rows_x * rows_y * rows_z * size_x * size_y)
-    lines = [v.reshape(rows_x * rows_y, rows_z) for v in (mass_scale, potential)]
-    node_values = jnp.concatenate(lines, axis=0)
-    node_values = jnp.concatenate([node_values] * 3, axis=1)
-    target_tile = jnp.pad(record_target[None, :], ((0, SLOT - 1), (0, STATES - CELLS)))
     padded = (ROWS + 1, ROWS + 1, COLUMN, STATES)
     inside = (ROWS, ROWS, COLUMN, STATES)
-    face = (ROWS, COLUMN, STATES)
+    pair = (PAIR, STATES)
+    face = (LINES,) + pair
     line = (COLUMN, STATES)
     share = STATES // size_y
     messages = 2 * size_y + size_x - 3
     vmem = pl.BlockSpec(memory_space=pltpu.VMEM)
-    return pl.pallas_call(
+    filtered, inverse, gram_matrix = pl.pallas_call(
         functools.partial(filter_kernel, size_x, size_y, node_total),
         out_shape=(
             jax.ShapeDtypeStruct((rows_x, rows_y, rows_z, STATES), F32),
             jax.ShapeDtypeStruct((STATES, STATES), F32),
+            jax.ShapeDtypeStruct((STATES, STATES), F32),
         ),
         in_specs=[pl.BlockSpec(memory_space=pltpu.SMEM)] * 2 + [vmem] * 5,
-        out_specs=(vmem, vmem),
+        out_specs=(pl.BlockSpec(memory_space=pl.ANY), vmem, vmem),
         scratch_shapes=[
             pltpu.VMEM(padded, F32),
             pltpu.VMEM(inside, F32),
             pltpu.VMEM((KDIM, SLOT * FACE), BF16),
             pltpu.VMEM((KDIM, 2 * FACE), BF16),
-            pltpu.VMEM((KDIM, 2 * FACE), BF16),
-            pltpu.VMEM((KDIM, 2 * FACE), BF16),
+            pltpu.VMEM((KDIM, FACE), BF16),
+            pltpu.VMEM((PAIR, 2 * COLUMN), BF16),
+            pltpu.VMEM((2 * COLUMN, PAIR), BF16),
+            pltpu.VMEM((2 * COLUMN, PAIR), BF16),
+            pltpu.VMEM((SLOT, STATES), jnp.int32),
+            pltpu.VMEM((rows_x, rows_y, rows_z, STATES), F32),
             pltpu.VMEM((3, CAPACITY, COARSE_ROWS, STATES), BF16),
             pltpu.VMEM((4 * CAPACITY, COARSE_ROWS, STATES), BF16),
             pltpu.VMEM((3, SLOT, STATES), jnp.int32),
@@ -695,15 +754,15 @@
             pltpu.VMEM((2 * FACE, COUNT_Z * STATES), BF16),
             pltpu.VMEM(face, BF16),
             pltpu.VMEM(face, BF16),
-            pltpu.VMEM((2, 2 * ORDER + POINTS) + line, BF16),
-            pltpu.VMEM((2, 3 * ORDER) + line, BF16),
+            pltpu.VMEM((2, LINES // 2 + LINES + 1) + pair, BF16),
+            pltpu.VMEM((2,) + face, BF16),
             pltpu.VMEM(face, BF16),
             pltpu.VMEM(face, BF16),
             pltpu.VMEM(line, BF16),
             pltpu.VMEM((2,) + face, BF16),
             pltpu.VMEM((2,) + face, BF16),
             pltpu.VMEM((2,) + line, BF16),
-            pltpu.VMEM((ROWS * ROWS * COLUMN, 2 * STATES), BF16),
+            pltpu.VMEM((ROWS * ROWS * DEPTH, 2 * STATES), BF16),
             pltpu.VMEM((STATES, STATES), F32),
             pltpu.VMEM((2, size_y - 1, share, STATES), F32),
             pltpu.VMEM((2, size_x, share, STATES), F32),
@@ -714,8 +773,9 @@
             pltpu.SemaphoreType.DMA((3,)),
             pltpu.SemaphoreType.DMA((3,)),
             pltpu.SemaphoreType.DMA((3,)),
-            pltpu.SemaphoreType.DMA((2, 8)),
-            pltpu.SemaphoreType.DMA((2, 8)),
+            pltpu.SemaphoreType.DMA,
+            pltpu.SemaphoreType.DMA((2, 7)),
+            pltpu.SemaphoreType.DMA((2, 7)),
             pltpu.SemaphoreType.DMA((2, messages)),
             pltpu.SemaphoreType.DMA((2, messages)),
         ],
@@ -726,7 +786,22 @@
             flops=6 * 4 * 2 * KDIM * KDIM * 512, bytes_accessed=10_000_000, transcendentals=0
         ),
         name="filter_twice",
-    )(filter_window, record_target, target_tile, coarse_states, padded_table(), node_values, cell_matrix)
+    )(
+        filter_window,
+        record_target,
+        coarse_states,
+        padded_table(),
+        mass_scale,
+        potential,
+        cell_matrix,
+    )
+    states = jnp.dot(
+        filtered.reshape(-1, STATES),
+        inverse.T,
+        precision=lax.Precision.HIGH,
+        preferred_element_type=F32,
+    )
+    return (states.reshape(filtered.shape), gram_matrix)
 
 
 def solution(mesh):

time: 136 us -> 131 us (0.963)
  Pallas kernels: 124 us -> 119 us
  matrix products: 0 us -> 3.55 us
  local copies, waits for them, and re-layouts: 10.2 us -> 6.73 us
    pallas_call x1, Pallas kernels: 124 us -> 119 us  [local(): pl.pallas_call(functools.partial(filter_kernel, size_x, size_y, node_tota...]
    dot_general x0 -> x1, matrix products: none -> 3.55 us  [local(): jnp.dot(filtered.reshape(-1, STATES), inverse.T, precision=lax.Precision....]
    reshape x2 -> x0, local copies, waits for them, and re-layouts: 1.8 us -> none  [local(): v.reshape(rows_x * rows_y, rows_z)]
    unnamed x11 -> x14, local copies, waits for them, and re-layouts: 7.74 us -> 6.73 us
where the time goes in v3:
time: 131 us; the launch traced here: 130 us
  Pallas kernels  119 us (91%)
  local copies, waits for them, and re-layouts  6.73 us (5%)
  matrix products  3.55 us (3%)
    pallas_call x1, Pallas kernels, local(): pl.pallas_call(functools.partial(filter_kernel, size_x, size_y, node_tota...  119 us
    unnamed x14, local copies, waits for them, and re-layouts  6.73 us
    dot_general x1, matrix products, local(): jnp.dot(filtered.reshape(-1, STATES), inverse.T, precision=lax.Precision....  3.55 us

profile of v3, /device:TPU:1, one launch (start us, length us, event | category | flops | bytes accessed | tf_op | source)
XLA Modules:
  0.0 130.3 jit_solution(11422694035108954171)
XLA Ops:
  0.6 1.2 copy.9.coarse
  1.8 0.0 copy-start
  1.8 0.9 copy-done
  2.8 0.0 copy-start.1
  2.8 0.9 copy-done.1
  3.7 0.0 copy-start.2
  3.7 0.9 copy-done.2
  4.5 0.0 copy-start.3
  4.5 0.7 copy-done.3
  5.2 0.0 copy-start.4
  5.2 0.7 copy-done.4
  5.9 0.0 copy-start.5
  5.9 0.9 copy-done.5
  6.7 119.3 %filter_twice.1 = (f32[12,12,24,128]{3,2,1,0:T(8,128)}, f32[128,128]{1,0:T(8,128)S(1)}, f32[128,128]{1,0:T(8,128)S(1)}) custom-call(f32[2]{0:T(128)S(1)} %copy-done.3, s32[16]{0:T(128)S(1)} %copy-done.4, bf16[16,125,128]{2,1,0:T(8,128)(2,1)S(1)} %copy.9.coarse, bf16[288,128]{1,0:T(8,128)(2,1)S(1)} %copy-done.5, f32[12,12,24]{2,1,0:T(8,128)S(1)} %copy-done.1, ...), custom_call_target="tpu_custom_call" | custom-call | flops 4932501504 | bytes 10000000 | tf_op jit(solution)/shard_map/filter_twice/pallas_call | solution.py:727
  126.1 3.6 %fusion = f32[12,12,24,128]{3,2,1,0:T(8,128)} fusion(f32[12,12,24,128]{3,2,1,0:T(8,128)} %get-tuple-element.5, f32[128,128]{1,0:T(8,128)S(1)} %get-tuple-element.6), kind=kOutput, calls=%fused_computation | convolution fusion | flops 339738624 | bytes 3604480 | tf_op jit(solution)/shard_map/dot_general | solution.py:798
  129.6 0.6 copy.12
Async XLA Ops:
  1.8 1.0 copy-start
  2.8 0.9 copy-start.1
  3.7 0.9 copy-start.2
  4.5 0.7 copy-start.3
  5.2 0.7 copy-start.4
  5.9 0.9 copy-start.5

commit v4 on v3

--- a/solution.py
+++ b/solution.py
@@ -49,6 +49,11 @@
     third = owned_rows[None, None, :, None, None, :]
     product = first * second * third
     return product.reshape(fine_degree**3, (coarse_degree + 1) ** 3)
+
+
+def cut_index(value, size):
+    assert size & (size - 1) == 0
+    return lax.shift_right_logical(value, size.bit_length() - 1), value & (size - 1)
 
 
 def row_in_slot(shape, axis):
@@ -125,10 +130,10 @@
     window,
     targets,
     coarse,
-    table,
-    mass_in,
-    pot_in,
-    cell_matrix,
+    table_any,
+    mass_any,
+    pot_any,
+    matrix_any,
     filtered_out,
     inverse_out,
     gram_out,
@@ -137,10 +142,15 @@
     matrix,
     from_x,
     from_y,
+    from_xy,
     shrink,
     grow,
     grow_own,
     target_tile,
+    table,
+    mass_in,
+    pot_in,
+    cell_matrix,
     filtered,
     slots,
     arrived,
@@ -149,6 +159,7 @@
     block,
     total,
     rhs,
+    rhs_two,
     rhs_taken,
     send_x,
     send_y,
@@ -172,6 +183,7 @@
     record_send,
     record_recv,
     store_sem,
+    fetch_sems,
     send_sems,
     recv_sems,
     sum_send,
@@ -188,26 +200,39 @@
     barrier = pltpu.get_barrier_semaphore()
     for partner in partners:
         pl.semaphore_signal(barrier, inc=1, device_id=partner, device_id_type=MESH)
+    fetches = [
+        pltpu.make_async_copy(src, dst, fetch_sems.at[i])
+        for i, (src, dst) in enumerate(
+            [
+                (matrix_any, cell_matrix),
+                (mass_any, mass_in),
+                (pot_any, pot_in),
+                (table_any, table),
+            ]
+        )
+    ]
+    for fetch in fetches:
+        fetch.start()
     steps = (None, (0, 1), (1, 0), (1, 1))
-    buckets, ranks = [], []
+    ranks = []
     counts = [0, 0, 0, 0]
     for r in range(CELLS):
-        device = targets[r] // CELLS
-        step_x = lax.rem(device // size_y - me_x + size_x, size_x)
-        step_y = lax.rem(lax.rem(device, size_y) - me_y + size_y, size_y)
+        device = cut_index(targets[r], CELLS)[0]
+        to_x, to_y = cut_index(device, size_y)
+        step_x = (to_x - me_x + size_x) & (size_x - 1)
+        step_y = (to_y - me_y + size_y) & (size_y - 1)
         bucket = 2 * step_x + step_y
         rank = 0
         for index in range(4):
-            rank = rank + jnp.where(bucket == index, counts[index], 0)
-            counts[index] = counts[index] + jnp.where(bucket == index, 1, 0)
-        buckets.append(bucket)
+            rank = jnp.where(bucket == index, counts[index], rank)
+            counts[index] = jnp.where(bucket == index, counts[index] + 1, counts[index])
         ranks.append(bucket * CAPACITY + rank)
 
     def record_of(slot):
         found = 0
         for r in range(CELLS):
-            found = found + jnp.where(ranks[r] == slot, r, 0)
-        return jnp.minimum(jnp.maximum(found, 0), CELLS - 1)
+            found = jnp.where(ranks[r] == slot, r, found)
+        return found & (CELLS - 1)
 
     last = COARSE_ROWS - 16
     for index in range(3):
@@ -246,8 +271,10 @@
     for k in range(CAPACITY):
         arrived[k, 0:coarse_count] = coarse[record_of(k)]
 
+    for fetch in fetches:
+        fetch.wait()
     place_nodes(mass_in, pot_in, mass, pot)
-    spread_matrix(cell_matrix, matrix, from_x, from_y)
+    spread_matrix(cell_matrix, matrix, from_x, from_y, from_xy)
     line_tables(shrink, grow, grow_own)
     block[1] = jnp.zeros(block.shape[1:], F32)
 
@@ -266,13 +293,14 @@
         seen = 0
         for r in range(CELLS):
             target = targets[r] if index == 0 else target_list[index - 1, 0, r]
-            hit = target // CELLS == own
-            cell = jnp.where(hit, lax.rem(target, CELLS), -1)
+            device, cell = cut_index(target, CELLS)
+            hit = device == own
+            cell = jnp.where(hit, cell, -1)
             slot = index * CAPACITY + seen
             for g in range(CELLS):
-                places[g] = places[g] + jnp.where(cell == g, slot, 0)
-            seen = seen + jnp.where(hit, 1, 0)
-    places = [jnp.minimum(jnp.maximum(p, 0), 4 * CAPACITY - 1) for p in places]
+                places[g] = jnp.where(cell == g, slot, places[g])
+            seen = jnp.where(hit, seen + 1, seen)
+    places = [p & (4 * CAPACITY - 1) for p in places]
     for index in (3, 2, 1):
         record_copies[index].wait()
     slot_row = row_in_slot((COLUMN, STATES), 0)
@@ -329,7 +357,7 @@
                     total[x, y, rows] = part
                 written.add((x, y))
 
-    def column(q, e, f, written):
+    def gather(q, e, f, out, lane):
         points_x = POINTS if e == 0 else ORDER
         for a in range(points_x):
             x = e * ORDER + a
@@ -346,10 +374,8 @@
                     copies = [a, POINTS] if (a == 0 and e == 0) else [a]
                     for place in copies:
                         first = (place * PAIRS + i) * 2 * SLOT
-                        rhs[first : first + 2 * SLOT, h * STATES : (h + 1) * STATES] = tile
-        depth = FACE * (SLOT if e == 0 else ORDER)
-        product = dot_nn(matrix[:, 0:depth], rhs[0:depth, :])
-        add_product(product, e, f, POINTS, POINTS, written)
+                        lanes = slice(lane + h * STATES, lane + (h + 1) * STATES)
+                        out[first : first + 2 * SLOT, lanes] = tile
 
     def taken_rows(base, lines, h):
         chunks = [line[h * SLOT : (h + 1) * SLOT] if line is not None else zeros for line in lines]
@@ -389,77 +415,108 @@
         first = row_in_slot(raw.shape, axis) == 0
         return raw + jnp.where(first, pltpu.roll(raw, SLOT - ORDER, axis), 0.0)
 
-    def finish(q, x, y, count, alpha, beta):
-        shape = (count, COLUMN, STATES)
-        slot_row = row_in_slot(shape, 1)
-        ys = pl.ds(y, count)
-        raw = total[x, ys]
+    def finish(q, index, alpha, beta):
+        raw = total[index]
+        slot_row = row_in_slot(raw.shape, 1)
         summed = folded(raw)
         again = pltpu.roll(summed, COLUMN - SLOT + ORDER, 1)
         full = jnp.where(slot_row < ORDER, summed, jnp.where(slot_row == ORDER, again, 0.0))
-        value = block[q, x, ys]
-        result = mass[x, ys] * full + (pot[x, ys] - center) * value
-        block[1 - q, x, ys] = alpha * result - beta * block[1 - q, x, ys]
+        value = block[(q,) + index]
+        result = mass[index] * full + (pot[index] - center) * value
+        block[(1 - q,) + index] = alpha * result - beta * block[(1 - q,) + index]
 
     def one_apply(k, p):
         q = lax.rem(p * CHEB_DEGREE + k, 2)
         first = k == 0
         alpha = jnp.where(first, 1.0, 2.0) / radius
         beta = jnp.where(first, 0.0, 1.0)
-        half = pl.ds(LINES // 2, LINES // 2)
         quarter = LINES // 2
-        values_x = [
+        half = pl.ds(quarter, quarter)
+        values = [
             remote(q, 0, send_x, take_x.at[q, pl.ds(quarter, LINES)], -1, 0),
-            remote(q, 2, send_x.at[half], take_x.at[q, pl.ds(0, quarter)], -1, 1),
+            remote(q, 1, send_x.at[half], take_x.at[q, pl.ds(0, quarter)], -1, 1),
             remote(
-                q, 3, send_x.at[pl.ds(0, 1)], take_x.at[q, pl.ds(quarter + LINES, 1)], -1, -1
+                q, 2, send_x.at[pl.ds(0, 1)], take_x.at[q, pl.ds(quarter + LINES, 1)], -1, -1
             ),
+            remote(q, 3, send_y.at[half], take_y.at[q, pl.ds(0, quarter)], 1, -1),
+            remote(q, 4, send_y, take_y.at[q, pl.ds(quarter, LINES)], 0, -1),
         ]
-        value_y = remote(q, 1, send_y, take_y.at[q], 0, -1)
-        sum_x = remote(q, 4, back_x, got_x.at[q], 1, 0)
-        sum_y = remote(q, 5, back_y, got_y.at[q], 0, 1)
-        sum_c = remote(q, 6, back_c, got_c.at[q], 1, 1)
+        sum_x = remote(q, 5, back_x, got_x.at[q], 1, 0)
+        sum_y = remote(q, 6, back_y, got_y.at[q], 0, 1)
+        sum_c = remote(q, 7, back_c, got_c.at[q], 1, 1)
         narrow(mass[0, 0:ROWS] * block[q, 0, 0:ROWS], send_x)
-        for copy in values_x:
+        for copy in values[0:3]:
             copy.start()
         narrow(mass[0:ROWS, 0] * block[q, 0:ROWS, 0], send_y)
-        value_y.start()
+        for copy in values[3:5]:
+            copy.start()
         written = set()
-        column(q, 1, 1, written)
-        column(q, 1, 0, written)
-        column(q, 0, 1, written)
+        width = COUNT_Z * STATES
+        inner = FACE * ORDER
+        gather(q, 1, 0, rhs_two, 0)
+        gather(q, 1, 1, rhs_two, width)
+        face = dot_nn(matrix[inner : inner + FACE, 0:inner], rhs_two[...])
+
+        def face_line(f, b):
+            parts = [
+                face[b * SLOT : (b + 1) * SLOT, f * width + h * STATES : f * width + (h + 1) * STATES]
+                for h in range(COUNT_Z)
+            ]
+            return jnp.concatenate(parts, axis=0)
+
+        lines = [face_line(0, b) for b in range(ORDER)]
+        lines.append(face_line(0, ORDER) + face_line(1, 0))
+        lines += [face_line(1, b) for b in range(1, ORDER)]
+        narrow(folded(jnp.stack(lines)), back_x)
+        sum_x.start()
+        back_c[...] = face_line(1, ORDER).astype(BF16)
+        sum_c.start()
+        product = dot_nn(matrix[0:inner, 0:inner], rhs_two[:, width : 2 * width])
+        add_product(product, 1, 1, ORDER, POINTS, written)
+        gather(q, 0, 1, rhs, 0)
+        add_product(dot_nn(matrix[...], rhs[...]), 0, 1, POINTS, POINTS, written)
         narrow(folded(total[0:ROWS, ROWS]), back_y)
         sum_y.start()
-        back_c[...] = total[ROWS, ROWS].astype(BF16)
-        sum_c.start()
-        value_y.wait()
-        along_y = widen([take_y[q, i] for i in range(LINES)], grow)
-        taken_column(1, 1, from_y, [along_y[ORDER:] + [None] * 2], POINTS, ORDER, written)
-        narrow(folded(total[ROWS, 0:ROWS]), back_x)
-        sum_x.start()
-        taken_column(
-            0, 1, from_y, [along_y[0:POINTS] + [along_y[0]]], POINTS, ORDER, written
-        )
-        column(q, 0, 0, written)
-        for copy in values_x:
+        product = dot_nn(matrix[0:inner, 0:inner], rhs_two[:, 0:width])
+        add_product(product, 1, 0, ORDER, POINTS, written)
+        gather(q, 0, 0, rhs, 0)
+        add_product(dot_nn(matrix[...], rhs[...]), 0, 0, POINTS, POINTS, written)
+        for copy in values:
             copy.wait()
         along_x = widen([take_x[q, i] for i in range(quarter + LINES + 1)], grow)
+        along_y = widen([take_y[q, i] for i in range(quarter + LINES)], grow)
         last = 2 * ORDER
+        none = [None]
         taken_column(
-            1, 1, from_x, [along_x[last : last + POINTS] + [None]], ORDER, ORDER, written
+            1,
+            1,
+            from_xy,
+            [along_x[last : last + POINTS] + none, along_y[last:] + none * 2],
+            ORDER,
+            ORDER,
+            written,
         )
         taken_column(
             1,
             0,
             from_x,
-            [along_x[ORDER : last + 1] + [None], along_x[0:POINTS] + [None]],
+            [along_x[ORDER : last + 1] + none, along_x[0:POINTS] + none],
             ORDER,
             POINTS,
             written,
         )
+        taken_column(
+            0,
+            1,
+            from_y,
+            [along_y[ORDER : last + 1] + none, along_y[0:POINTS] + none],
+            POINTS,
+            ORDER,
+            written,
+        )
 
         def interior(x, carry):
-            finish(q, x, 1, ROWS - 1, alpha, beta)
+            finish(q, (x, pl.ds(1, ROWS - 1)), alpha, beta)
             return carry
 
         lax.fori_loop(1, ROWS, interior, 0)
@@ -470,13 +527,8 @@
             total[x, 0] += line
         for y, line in enumerate(widen([got_x[q, i] for i in range(LINES)], grow_own)):
             total[0, y] += line
-        finish(q, 0, 0, ROWS, alpha, beta)
-
-        def edge(x, carry):
-            finish(q, x, 0, 1, alpha, beta)
-            return carry
-
-        lax.fori_loop(1, ROWS, edge, 0)
+        finish(q, (0, slice(0, ROWS)), alpha, beta)
+        finish(q, (slice(1, ROWS), 0), alpha, beta)
 
     def sum_everywhere(p):
         share = STATES // size_y
@@ -629,7 +681,7 @@
             out[x, 0:ROWS] = lines.reshape(ROWS, COLUMN, STATES)
         return carry
 
-    lax.fori_loop(0, ROWS, one, 0)
+    lax.fori_loop(0, ROWS, one, 0, unroll=2)
     mass[ROWS] = jnp.ones(mass.shape[1:], F32)
     mass[0:ROWS, ROWS] = jnp.ones((ROWS, COLUMN, STATES), F32)
 
@@ -649,7 +701,7 @@
     grow_own[...] = jnp.where(same & (c < ORDER), 1.0, 0.0).astype(BF16)
 
 
-def spread_matrix(cell_matrix, matrix, from_x, from_y):
+def spread_matrix(cell_matrix, matrix, from_x, from_y, from_xy):
     nodes = POINTS**3
     row = lax.broadcasted_iota(jnp.int32, (KDIM, nodes), 0)
     col = lax.broadcasted_iota(jnp.int32, (KDIM, nodes), 1)
@@ -688,6 +740,7 @@
     face_y = jnp.where(row == (col // SLOT) * FACE + ORDER * SLOT + col % SLOT, 1.0, 0.0)
     faces = jnp.concatenate([face_x, face_y], axis=1).astype(BF16)
     both = dot_nn(full[:, 0:KDIM].astype(BF16), faces)
+    from_xy[...] = both.astype(BF16)
     low = lax.broadcasted_iota(jnp.int32, (FACE, 2 * FACE), 1) < FACE
     groups = []
     for a in range(POINTS):
@@ -697,11 +750,12 @@
         )
         groups.append(jnp.where(low, group, pltpu.roll(moved, FACE, 1)))
     from_x[...] = jnp.concatenate(groups, axis=0).astype(BF16)
-    faces_y = pltpu.roll(both, FACE, 1)[:, 0:FACE]
-    seen_y = pltpu.roll(both[ORDER * FACE : POINTS * FACE], FACE + SLOT, 1)[:, 0:FACE]
-    at_end = lax.broadcasted_iota(jnp.int32, (FACE, FACE), 1) >= POINTS * SLOT
-    first = jnp.where(at_end, seen_y, faces_y[0:FACE])
-    from_y[...] = jnp.concatenate([first, faces_y[FACE:]], axis=0).astype(BF16)
+    groups = []
+    for a in range(POINTS):
+        group = pltpu.roll(both[a * FACE : (a + 1) * FACE], FACE, 1)
+        moved = both[ORDER * FACE : POINTS * FACE] if a == 0 else jnp.zeros_like(group)
+        groups.append(jnp.where(low, group, moved))
+    from_y[...] = jnp.concatenate(groups, axis=0).astype(BF16)
 
 
 def padded_table():
@@ -731,18 +785,25 @@
             jax.ShapeDtypeStruct((STATES, STATES), F32),
             jax.ShapeDtypeStruct((STATES, STATES), F32),
         ),
-        in_specs=[pl.BlockSpec(memory_space=pltpu.SMEM)] * 2 + [vmem] * 5,
+        in_specs=[pl.BlockSpec(memory_space=pltpu.SMEM)] * 2
+        + [vmem]
+        + [pl.BlockSpec(memory_space=pl.ANY)] * 4,
         out_specs=(pl.BlockSpec(memory_space=pl.ANY), vmem, vmem),
         scratch_shapes=[
             pltpu.VMEM(padded, F32),
             pltpu.VMEM(inside, F32),
             pltpu.VMEM((KDIM, SLOT * FACE), BF16),
             pltpu.VMEM((KDIM, 2 * FACE), BF16),
-            pltpu.VMEM((KDIM, FACE), BF16),
+            pltpu.VMEM((KDIM, 2 * FACE), BF16),
+            pltpu.VMEM((KDIM, 2 * FACE), BF16),
             pltpu.VMEM((PAIR, 2 * COLUMN), BF16),
             pltpu.VMEM((2 * COLUMN, PAIR), BF16),
             pltpu.VMEM((2 * COLUMN, PAIR), BF16),
             pltpu.VMEM((SLOT, STATES), jnp.int32),
+            pltpu.VMEM((ORDER * ORDER * SLOT, COARSE_ROWS), BF16),
+            pltpu.VMEM(mass_scale.shape, F32),
+            pltpu.VMEM(potential.shape, F32),
+            pltpu.VMEM(cell_matrix.shape, BF16),
             pltpu.VMEM((rows_x, rows_y, rows_z, STATES), F32),
             pltpu.VMEM((3, CAPACITY, COARSE_ROWS, STATES), BF16),
             pltpu.VMEM((4 * CAPACITY, COARSE_ROWS, STATES), BF16),
@@ -751,11 +812,12 @@
             pltpu.VMEM((2,) + padded, F32),
             pltpu.VMEM(padded, F32),
             pltpu.VMEM((SLOT * FACE, COUNT_Z * STATES), BF16),
+            pltpu.VMEM((ORDER * FACE, 2 * COUNT_Z * STATES), BF16),
             pltpu.VMEM((2 * FACE, COUNT_Z * STATES), BF16),
             pltpu.VMEM(face, BF16),
             pltpu.VMEM(face, BF16),
             pltpu.VMEM((2, LINES // 2 + LINES + 1) + pair, BF16),
-            pltpu.VMEM((2,) + face, BF16),
+            pltpu.VMEM((2, LINES // 2 + LINES) + pair, BF16),
             pltpu.VMEM(face, BF16),
             pltpu.VMEM(face, BF16),
             pltpu.VMEM(line, BF16),
@@ -774,8 +836,9 @@
             pltpu.SemaphoreType.DMA((3,)),
             pltpu.SemaphoreType.DMA((3,)),
             pltpu.SemaphoreType.DMA,
-            pltpu.SemaphoreType.DMA((2, 7)),
-            pltpu.SemaphoreType.DMA((2, 7)),
+            pltpu.SemaphoreType.DMA((4,)),
+            pltpu.SemaphoreType.DMA((2, 8)),
+            pltpu.SemaphoreType.DMA((2, 8)),
             pltpu.SemaphoreType.DMA((2, messages)),
             pltpu.SemaphoreType.DMA((2, messages)),
         ],

time: 131 us -> 129 us (0.985)
    pallas_call x1, Pallas kernels: 119 us -> 118 us  [local(): pl.pallas_call(functools.partial(filter_kernel, size_x, size_y, node_tota...]
where the time goes in v4:
time: 129 us
  Pallas kernels  118 us (91%)
  local copies, waits for them, and re-layouts  6.73 us (5%)
  matrix products  3.55 us (3%)
    pallas_call x1, Pallas kernels, local(): pl.pallas_call(functools.partial(filter_kernel, size_x, size_y, node_tota...  118 us
    unnamed x14, local copies, waits for them, and re-layouts  6.73 us
    dot_general x1, matrix products, local(): jnp.dot(filtered.reshape(-1, STATES), inverse.T, precision=lax.Precision....  3.55 us

profile of v4, /device:TPU:1, one launch (start us, length us, event | category | flops | bytes accessed | tf_op | source)
XLA Modules:
  0.0 128.7 jit_solution(10702173093907283795)
XLA Ops:
  0.6 1.2 copy.9.coarse
  1.8 0.0 copy-start
  1.8 0.9 copy-done
  2.8 0.0 copy-start.1
  2.8 0.9 copy-done.1
  3.7 0.0 copy-start.2
  3.7 0.9 copy-done.2
  4.5 0.0 copy-start.3
  4.5 0.7 copy-done.3
  5.2 0.0 copy-start.4
  5.2 0.7 copy-done.4
  5.9 0.0 copy-start.5
  5.9 0.9 copy-done.5
  6.7 117.8 %filter_twice.1 = (f32[12,12,24,128]{3,2,1,0:T(8,128)}, f32[128,128]{1,0:T(8,128)S(1)}, f32[128,128]{1,0:T(8,128)S(1)}) custom-call(f32[2]{0:T(128)S(1)} %copy-done.3, s32[16]{0:T(128)S(1)} %copy-done.4, bf16[16,125,128]{2,1,0:T(8,128)(2,1)S(1)} %copy.9.coarse, bf16[288,128]{1,0:T(8,128)(2,1)S(1)} %copy-done.5, f32[12,12,24]{2,1,0:T(8,128)S(1)} %copy-done.1, ...), custom_call_target="tpu_custom_call" | custom-call | flops 4932501504 | bytes 10000000 | tf_op jit(solution)/shard_map/filter_twice/pallas_call | solution.py:781
  124.5 3.6 %fusion = f32[12,12,24,128]{3,2,1,0:T(8,128)} fusion(f32[12,12,24,128]{3,2,1,0:T(8,128)} %get-tuple-element.5, f32[128,128]{1,0:T(8,128)S(1)} %get-tuple-element.6), kind=kOutput, calls=%fused_computation | convolution fusion | flops 339738624 | bytes 3604480 | tf_op jit(solution)/shard_map/dot_general | solution.py:861
  128.1 0.6 copy.12
Async XLA Ops:
  1.8 1.0 copy-start
  2.8 0.9 copy-start.1
  3.7 0.9 copy-start.2
  4.5 0.7 copy-start.3
  5.2 0.7 copy-start.4
  5.9 0.9 copy-start.5

commit v5 on v4

--- a/solution.py
+++ b/solution.py
@@ -24,6 +24,7 @@
 PAIR = 2 * DEPTH
 LINES = ROWS // 2
 CELLS = 16
+PANEL = 16
 CAPACITY = CELLS // 2
 COARSE_ROWS = 128
 MESH = pl.DeviceIdType.MESH
@@ -86,32 +87,31 @@
 
 def factor_rows(work):
     size = STATES
-    sub = lax.broadcasted_iota(jnp.int32, (SLOT, size), 0)
-    lane = lax.broadcasted_iota(jnp.int32, (SLOT, size), 1)
+    sub = lax.broadcasted_iota(jnp.int32, (PANEL, size), 0)
+    lane = lax.broadcasted_iota(jnp.int32, (PANEL, size), 1)
 
     def panel(j, carry):
-        base = pl.multiple_of(j * SLOT, SLOT)
-        left = work[pl.ds(base, SLOT), 0:size]
-        right = work[pl.ds(base, SLOT), size : 2 * size]
+        base = pl.multiple_of(j * PANEL, PANEL)
+        left = work[pl.ds(base, PANEL), 0:size]
+        right = work[pl.ds(base, PANEL), size : 2 * size]
         turned = pltpu.roll(left, lax.rem(size - base, size), 1)
-        columns = [jnp.broadcast_to(turned[:, m : m + 1], (SLOT, size)) for m in range(SLOT)]
-        for m in range(SLOT):
-            pivot = jnp.broadcast_to(columns[m][m : m + 1, :], (SLOT, size))
+        columns = [jnp.broadcast_to(turned[:, m : m + 1], (PANEL, size)) for m in range(PANEL)]
+        for m in range(PANEL):
+            pivot = jnp.broadcast_to(columns[m][m : m + 1, :], (PANEL, size))
             scale = lax.rsqrt(pivot)
-            scale = scale * (1.5 - 0.5 * pivot * scale * scale)
             below = sub > m
             at = sub == m
             coef = columns[m] * scale
-            row_left = jnp.broadcast_to(left[m : m + 1, :], (SLOT, size)) * scale
-            row_right = jnp.broadcast_to(right[m : m + 1, :], (SLOT, size)) * scale
-            for n in range(m + 1, SLOT):
-                entry = jnp.broadcast_to(columns[n][m : m + 1, :], (SLOT, size)) * scale
+            row_left = jnp.broadcast_to(left[m : m + 1, :], (PANEL, size)) * scale
+            row_right = jnp.broadcast_to(right[m : m + 1, :], (PANEL, size)) * scale
+            for n in range(m + 1, PANEL):
+                entry = jnp.broadcast_to(columns[n][m : m + 1, :], (PANEL, size)) * scale
                 columns[n] = jnp.where(below, columns[n] - coef * entry, columns[n])
             left = jnp.where(below, left - coef * row_left, jnp.where(at, row_left, left))
             right = jnp.where(below, right - coef * row_right, jnp.where(at, row_right, right))
-        work[pl.ds(base, SLOT), 0:size] = left
-        work[pl.ds(base, SLOT), size : 2 * size] = right
-        later = jnp.where(lane >= base + SLOT, left, 0.0)
+        work[pl.ds(base, PANEL), 0:size] = left
+        work[pl.ds(base, PANEL), size : 2 * size] = right
+        later = jnp.where(lane >= base + PANEL, left, 0.0)
         l1, l2, l3 = [v.astype(F32) for v in split_three(later)]
         both = jnp.concatenate([left, right], axis=1)
         b1, b2, b3 = [v.astype(F32) for v in split_three(both)]
@@ -120,7 +120,7 @@
         work[...] = work[...] - dot_tn(lhs, rhs)
         return carry
 
-    lax.fori_loop(0, size // SLOT, panel, 0)
+    lax.fori_loop(0, size // PANEL, panel, 0)
 
 
 def filter_kernel(
@@ -151,7 +151,6 @@
     mass_in,
     pot_in,
     cell_matrix,
-    filtered,
     slots,
     arrived,
     target_in,
@@ -425,9 +424,9 @@
         result = mass[index] * full + (pot[index] - center) * value
         block[(1 - q,) + index] = alpha * result - beta * block[(1 - q,) + index]
 
-    def one_apply(k, p):
-        q = lax.rem(p * CHEB_DEGREE + k, 2)
-        first = k == 0
+    def one_apply(t):
+        q = t % 2
+        first = (t % CHEB_DEGREE) == 0
         alpha = jnp.where(first, 1.0, 2.0) / radius
         beta = jnp.where(first, 0.0, 1.0)
         quarter = LINES // 2
@@ -481,6 +480,15 @@
         add_product(product, 1, 0, ORDER, POINTS, written)
         gather(q, 0, 0, rhs, 0)
         add_product(dot_nn(matrix[...], rhs[...]), 0, 0, POINTS, POINTS, written)
+
+        @pl.when(t == CHEB_DEGREE)
+        def _():
+            gather_pieces(0)
+
+        @pl.when(t == CHEB_DEGREE + 1)
+        def _():
+            gather_rows(0)
+
         for copy in values:
             copy.wait()
         along_x = widen([take_x[q, i] for i in range(quarter + LINES + 1)], grow)
@@ -530,122 +538,126 @@
         finish(q, (0, slice(0, ROWS)), alpha, beta)
         finish(q, (slice(1, ROWS), 0), alpha, beta)
 
-    def sum_everywhere(p):
-        share = STATES // size_y
-
-        def move(index, src, dst, device):
-            return pltpu.make_async_remote_copy(
-                src_ref=src,
-                dst_ref=dst,
-                send_sem=sum_send.at[p, index],
-                recv_sem=sum_recv.at[p, index],
-                device_id=device,
-                device_id_type=MESH,
-            )
-
-        def rows_of(owner):
-            return pl.ds(pl.multiple_of(owner * share, SLOT), share)
-
-        mine = rows_of(me_y)
+    share = STATES // size_y
+
+    def move(p, index, src, dst, device):
+        return pltpu.make_async_remote_copy(
+            src_ref=src,
+            dst_ref=dst,
+            send_sem=sum_send.at[p, index],
+            recv_sem=sum_recv.at[p, index],
+            device_id=device,
+            device_id_type=MESH,
+        )
+
+    def rows_of(owner):
+        return pl.ds(pl.multiple_of(owner * share, SLOT), share)
+
+    mine = rows_of(me_y)
+
+    def piece_copies(p):
         copies = []
         for d in range(1, size_y):
             device = at(0, d)
-            copies.append(
-                move(d - 1, partial.at[rows_of(device[1])], piece_in.at[p, d - 1], device)
-            )
-        for copy in copies:
-            copy.start()
-        for copy in copies:
+            src = partial.at[rows_of(device[1])]
+            copies.append(move(p, d - 1, src, piece_in.at[p, d - 1], device))
+        return copies
+
+    def ring_copies(p):
+        own = ring_in.at[p, me_x]
+        return [move(p, size_y + d - 2, own, own, at(d, 0)) for d in range(1, size_x)]
+
+    def row_copies(p):
+        own = gram_sum.at[p, mine]
+        first = size_y + size_x - 3
+        return [move(p, first + d, own, own, at(0, d)) for d in range(1, size_y)]
+
+    def gather_pieces(p):
+        for copy in piece_copies(p):
             copy.wait()
         piece = partial[mine, :]
         for d in range(1, size_y):
             piece = piece + piece_in[p, d - 1]
         ring_in[p, me_x] = piece
-        copies = []
-        for d in range(1, size_x):
-            copies.append(
-                move(size_y + d - 2, ring_in.at[p, me_x], ring_in.at[p, me_x], at(d, 0))
-            )
-        for copy in copies:
+        for copy in ring_copies(p):
             copy.start()
-        for copy in copies:
+
+    def gather_rows(p):
+        for copy in ring_copies(p):
             copy.wait()
         piece = ring_in[p, 0]
         for d in range(1, size_x):
             piece = piece + ring_in[p, d]
         gram_sum[p, mine] = piece / node_total
-        copies = []
-        for d in range(1, size_y):
-            copies.append(
-                move(
-                    size_y + size_x + d - 3, gram_sum.at[p, mine], gram_sum.at[p, mine], at(0, d)
-                )
-            )
-        for copy in copies:
+        for copy in row_copies(p):
             copy.start()
-        for copy in copies:
-            copy.wait()
-
-    def one_pass(p, carry):
-        def step(k, inner):
-            one_apply(k, p)
-            return inner
-
-        lax.fori_loop(0, CHEB_DEGREE, step, 0)
-        q = lax.rem((p + 1) * CHEB_DEGREE, 2)
-
+
+    def begin_sum(p, q):
         def divide(x, inner):
             value = block[q, x, 0:ROWS]
             value = jnp.concatenate(
                 [value[:, h * SLOT : h * SLOT + ORDER] for h in range(COUNT_Z)], axis=1
             )
-
-            @pl.when(p == 1)
-            def _():
-                filtered[x] = value
-
             high_part, low_part = split_two(value.reshape(ROWS * DEPTH, STATES))
             rows = pl.ds(pl.multiple_of(x * ROWS * DEPTH, ROWS * DEPTH), ROWS * DEPTH)
             split[rows, 0:STATES] = high_part
             split[rows, STATES : 2 * STATES] = low_part
+            split[rows, 2 * STATES : 3 * STATES] = high_part
             return inner
 
         lax.fori_loop(0, ROWS, divide, 0)
-
-        @pl.when(p == 1)
-        def _():
-            pltpu.make_async_copy(filtered, filtered_out, store_sem).start()
-
-        products = dot_tn(split[:, 0:STATES], split[...])
+        products = dot_tn(split[:, 0:STATES], split[:, 0 : 2 * STATES])
         cross = products[:, STATES : 2 * STATES]
         partial[...] = products[:, 0:STATES] + cross + cross.T
-        sum_everywhere(p)
-        whole = gram_sum[p]
-        work[:, 0:STATES] = whole
-        diagonal = lax.broadcasted_iota(jnp.int32, (STATES, STATES), 0) == lax.broadcasted_iota(
-            jnp.int32, (STATES, STATES), 1
+        for copy in piece_copies(p):
+            copy.start()
+
+    def end_sum(p):
+        for copy in row_copies(p):
+            copy.wait()
+        work[:, 0:STATES] = gram_sum[p]
+        shape = (STATES, STATES)
+        diagonal = lax.broadcasted_iota(jnp.int32, shape, 0) == lax.broadcasted_iota(
+            jnp.int32, shape, 1
         )
         work[:, STATES : 2 * STATES] = jnp.where(diagonal, 1.0, 0.0)
         factor_rows(work)
-        inverse = work[:, STATES : 2 * STATES]
-        gram_out[...] = whole
-        inverse_out[...] = inverse
-
-        @pl.when(p == 0)
+        return work[:, STATES : 2 * STATES]
+
+    def step(t, carry):
+        @pl.when(t == CHEB_DEGREE)
         def _():
-            pair = stacked_inverse(inverse)
+            begin_sum(0, CHEB_DEGREE % 2)
+
+        one_apply(t)
+
+        @pl.when(t == CHEB_DEGREE + 1)
+        def _():
+            pair = stacked_inverse(end_sum(0))
 
             def turn(x, inner):
-                value = block[q, x, 0:ROWS].reshape(ROWS * COLUMN, STATES)
-                block[q, x, 0:ROWS] = times_inverse(value, pair).reshape(ROWS, COLUMN, STATES)
+                for index in range(2):
+                    value = block[index, x, 0:ROWS].reshape(ROWS * COLUMN, STATES)
+                    block[index, x, 0:ROWS] = times_inverse(value, pair).reshape(
+                        ROWS, COLUMN, STATES
+                    )
                 return inner
 
             lax.fori_loop(0, ROWS, turn, 0)
 
         return carry
 
-    lax.fori_loop(0, 2, one_pass, 0)
-    pltpu.make_async_copy(filtered, filtered_out, store_sem).wait()
+    lax.fori_loop(0, 2 * CHEB_DEGREE, step, 0)
+    begin_sum(1, 0)
+    store = pltpu.make_async_copy(split, filtered_out, store_sem)
+    store.start()
+    gather_pieces(1)
+    gather_rows(1)
+    inverse = end_sum(1)
+    high_part, low_part = split_two(inverse)
+    inverse_out[...] = jnp.concatenate([high_part, high_part, low_part], axis=1)
+    gram_out[...] = gram_sum[1]
+    store.wait()
 
 
 def stacked_inverse(inverse):
@@ -781,8 +793,8 @@
     filtered, inverse, gram_matrix = pl.pallas_call(
         functools.partial(filter_kernel, size_x, size_y, node_total),
         out_shape=(
-            jax.ShapeDtypeStruct((rows_x, rows_y, rows_z, STATES), F32),
-            jax.ShapeDtypeStruct((STATES, STATES), F32),
+            jax.ShapeDtypeStruct((rows_x * rows_y * rows_z, 3 * STATES), BF16),
+            jax.ShapeDtypeStruct((STATES, 3 * STATES), BF16),
             jax.ShapeDtypeStruct((STATES, STATES), F32),
         ),
         in_specs=[pl.BlockSpec(memory_space=pltpu.SMEM)] * 2
@@ -804,7 +816,6 @@
             pltpu.VMEM(mass_scale.shape, F32),
             pltpu.VMEM(potential.shape, F32),
             pltpu.VMEM(cell_matrix.shape, BF16),
-            pltpu.VMEM((rows_x, rows_y, rows_z, STATES), F32),
             pltpu.VMEM((3, CAPACITY, COARSE_ROWS, STATES), BF16),
             pltpu.VMEM((4 * CAPACITY, COARSE_ROWS, STATES), BF16),
             pltpu.VMEM((3, SLOT, STATES), jnp.int32),
@@ -824,7 +835,7 @@
             pltpu.VMEM((2,) + face, BF16),
             pltpu.VMEM((2,) + face, BF16),
             pltpu.VMEM((2,) + line, BF16),
-            pltpu.VMEM((ROWS * ROWS * DEPTH, 2 * STATES), BF16),
+            pltpu.VMEM((ROWS * ROWS * DEPTH, 3 * STATES), BF16),
             pltpu.VMEM((STATES, STATES), F32),
             pltpu.VMEM((2, size_y - 1, share, STATES), F32),
             pltpu.VMEM((2, size_x, share, STATES), F32),
@@ -843,7 +854,7 @@
             pltpu.SemaphoreType.DMA((2, messages)),
         ],
         compiler_params=pltpu.CompilerParams(
-            collective_id=0, has_side_effects=True, vmem_limit_bytes=52 * 1024 * 1024
+            collective_id=0, has_side_effects=True, vmem_limit_bytes=62 * 1024 * 1024
         ),
         cost_estimate=pl.CostEstimate(
             flops=6 * 4 * 2 * KDIM * KDIM * 512, bytes_accessed=10_000_000, transcendentals=0
@@ -858,13 +869,8 @@
         potential,
         cell_matrix,
     )
-    states = jnp.dot(
-        filtered.reshape(-1, STATES),
-        inverse.T,
-        precision=lax.Precision.HIGH,
-        preferred_element_type=F32,
-    )
-    return (states.reshape(filtered.shape), gram_matrix)
+    states = dot_nt(filtered, inverse)
+    return (states.reshape(rows_x, rows_y, rows_z, STATES), gram_matrix)
 
 
 def solution(mesh):

time: 129 us -> 109 us (0.84)
  Pallas kernels: 118 us -> 101 us
  local copies, waits for them, and re-layouts: 6.73 us -> 2.6 us
    pallas_call x1, Pallas kernels: 118 us -> 101 us  [local(): pl.pallas_call(functools.partial(filter_kernel, size_x, size_y, node_tota...]
    unnamed x14 -> x4, local copies, waits for them, and re-layouts: 6.73 us -> 2.6 us
where the time goes in v5:
time: 109 us
  Pallas kernels  101 us (93%)
  matrix products  3.85 us (4%)
  local copies, waits for them, and re-layouts  2.6 us (2%)
    pallas_call x1, Pallas kernels, local(): pl.pallas_call(functools.partial(filter_kernel, size_x, size_y, node_tota...  101 us
    dot_general x1, matrix products, dot_nt(): lax.dot_general(a, b, (((1,), (1,)), ((), ())), preferred_element_type=F32)  3.85 us
    unnamed x4, local copies, waits for them, and re-layouts  2.6 us

profile of v5, /device:TPU:1, one launch (start us, length us, event | category | flops | bytes accessed | tf_op | source)
XLA Modules:
  0.0 108.5 jit_solution(9263619016162581991)
XLA Ops:
  0.6 2.0 %copy.9.coarse = bf16[16,125,128]{2,1,0:T(8,128)(2,1)} copy(bf16[16,125,128]{2,0,1:T(8,128)(2,1)} %param.7) | data formatting | bytes 1024000 | tf_op args[0]
  2.6 101.4 %filter_twice.1 = (bf16[3456,384]{1,0:T(8,128)(2,1)}, bf16[128,384]{1,0:T(8,128)(2,1)}, f32[128,128]{1,0:T(8,128)}) custom-call(f32[2]{0:T(128)} %window.1, s32[16]{0:T(128)} %targets.1, bf16[16,125,128]{2,1,0:T(8,128)(2,1)} %copy.9.coarse, bf16[288,128]{1,0:T(8,128)(2,1)} %constant.7.table_any, f32[12,12,24]{2,1,0:T(8,128)} %mass_any.1, ...), custom_call_target="tpu_custom_call" | custom-call | flops 4932501504 | bytes 10000000 | tf_op jit(solution)/shard_map/filter_twice/pallas_call | solution.py:793
  104.0 0.0 copy-start
  104.0 3.8 %fusion = f32[3456,128]{1,0:T(8,128)} fusion(bf16[3456,384]{1,0:T(8,128)(2,1)} %get-tuple-element.5, bf16[128,384]{1,0:T(8,128)(2,1)} %get-tuple-element.6), kind=kOutput, calls=%fused_computation | convolution fusion | flops 339738624 | bytes 4521984 | tf_op jit(solution)/shard_map/dot_general | solution.py:73
  107.9 0.0 copy-done
  107.9 0.6 copy.11
Async XLA Ops:
  104.0 3.9 %copy-start = (f32[128,128]{1,0:T(8,128)S(1)}, f32[128,128]{1,0:T(8,128)}, u32[]{:S(2)}) copy-start(f32[128,128]{1,0:T(8,128)} %get-tuple-element.11) | copy-start | bytes 196612

commit v6 on v5

--- a/solution.py
+++ b/solution.py
@@ -89,13 +89,13 @@
     size = STATES
     sub = lax.broadcasted_iota(jnp.int32, (PANEL, size), 0)
     lane = lax.broadcasted_iota(jnp.int32, (PANEL, size), 1)
-
-    def panel(j, carry):
-        base = pl.multiple_of(j * PANEL, PANEL)
-        left = work[pl.ds(base, PANEL), 0:size]
-        right = work[pl.ds(base, PANEL), size : 2 * size]
-        turned = pltpu.roll(left, lax.rem(size - base, size), 1)
-        columns = [jnp.broadcast_to(turned[:, m : m + 1], (PANEL, size)) for m in range(PANEL)]
+    for base in range(0, size, PANEL):
+        end = base + PANEL
+        left = work[base:end, 0:size]
+        right = work[base:end, size : 2 * size]
+        columns = [
+            jnp.broadcast_to(left[:, base + m : base + m + 1], (PANEL, size)) for m in range(PANEL)
+        ]
         for m in range(PANEL):
             pivot = jnp.broadcast_to(columns[m][m : m + 1, :], (PANEL, size))
             scale = lax.rsqrt(pivot)
@@ -109,18 +109,16 @@
                 columns[n] = jnp.where(below, columns[n] - coef * entry, columns[n])
             left = jnp.where(below, left - coef * row_left, jnp.where(at, row_left, left))
             right = jnp.where(below, right - coef * row_right, jnp.where(at, row_right, right))
-        work[pl.ds(base, PANEL), 0:size] = left
-        work[pl.ds(base, PANEL), size : 2 * size] = right
-        later = jnp.where(lane >= base + PANEL, left, 0.0)
-        l1, l2, l3 = [v.astype(F32) for v in split_three(later)]
-        both = jnp.concatenate([left, right], axis=1)
-        b1, b2, b3 = [v.astype(F32) for v in split_three(both)]
-        lhs = jnp.concatenate([l1, l1, l2, l1, l3, l2], axis=0).astype(BF16)
-        rhs = jnp.concatenate([b1, b2, b1, b3, b1, b2], axis=0).astype(BF16)
-        work[...] = work[...] - dot_tn(lhs, rhs)
-        return carry
-
-    lax.fori_loop(0, size // PANEL, panel, 0)
+        work[base:end, 0:size] = left
+        work[base:end, size : 2 * size] = right
+        if end < size:
+            later = jnp.where(lane >= end, left, 0.0)
+            l1, l2, l3 = [v.astype(F32) for v in split_three(later)]
+            both = jnp.concatenate([left, right], axis=1)
+            b1, b2, b3 = [v.astype(F32) for v in split_three(both)]
+            lhs = jnp.concatenate([l1, l1, l2, l1, l3, l2], axis=0).astype(BF16)
+            rhs = jnp.concatenate([b1, b2, b1, b3, b1, b2], axis=0).astype(BF16)
+            work[end:size, :] = work[end:size, :] - dot_tn(lhs, rhs)[end:size, :]
 
 
 def filter_kernel(
@@ -446,9 +444,6 @@
         narrow(mass[0, 0:ROWS] * block[q, 0, 0:ROWS], send_x)
         for copy in values[0:3]:
             copy.start()
-        narrow(mass[0:ROWS, 0] * block[q, 0:ROWS, 0], send_y)
-        for copy in values[3:5]:
-            copy.start()
         written = set()
         width = COUNT_Z * STATES
         inner = FACE * ORDER
@@ -470,6 +465,9 @@
         sum_x.start()
         back_c[...] = face_line(1, ORDER).astype(BF16)
         sum_c.start()
+        narrow(mass[0:ROWS, 0] * block[q, 0:ROWS, 0], send_y)
+        for copy in values[3:5]:
+            copy.start()
         product = dot_nn(matrix[0:inner, 0:inner], rhs_two[:, width : 2 * width])
         add_product(product, 1, 1, ORDER, POINTS, written)
         gather(q, 0, 1, rhs, 0)
@@ -489,17 +487,25 @@
         def _():
             gather_rows(0)
 
-        for copy in values:
+        last = 2 * ORDER
+        none = [None]
+        values[4].wait()
+        along_y = widen([take_y[q, i] for i in range(quarter, quarter + LINES)], grow)
+        taken_column(0, 1, from_y, [along_y[0:POINTS] + none], POINTS, ORDER, written)
+
+        def interior(x, carry):
+            finish(q, (x, pl.ds(1, ROWS - 1)), alpha, beta)
+            return carry
+
+        lax.fori_loop(1, ORDER, interior, 0)
+        for copy in values[0:4]:
             copy.wait()
         along_x = widen([take_x[q, i] for i in range(quarter + LINES + 1)], grow)
-        along_y = widen([take_y[q, i] for i in range(quarter + LINES)], grow)
-        last = 2 * ORDER
-        none = [None]
         taken_column(
             1,
             1,
             from_xy,
-            [along_x[last : last + POINTS] + none, along_y[last:] + none * 2],
+            [along_x[last : last + POINTS] + none, along_y[ORDER:] + none * 2],
             ORDER,
             ORDER,
             written,
@@ -513,21 +519,12 @@
             POINTS,
             written,
         )
-        taken_column(
-            0,
-            1,
-            from_y,
-            [along_y[ORDER : last + 1] + none, along_y[0:POINTS] + none],
-            POINTS,
-            ORDER,
-            written,
-        )
-
-        def interior(x, carry):
-            finish(q, (x, pl.ds(1, ROWS - 1)), alpha, beta)
-            return carry
-
-        lax.fori_loop(1, ROWS, interior, 0)
+        lax.fori_loop(ORDER, ROWS, interior, 0)
+        behind_y = widen([take_y[q, i] for i in range(quarter)], grow)
+        for h in range(COUNT_Z):
+            taken_rows(0, behind_y + [along_y[0]] + none, h)
+        product = dot_nn(from_y[0:FACE, FACE : 2 * FACE], rhs_taken[0:FACE, :])
+        add_product(product, 0, 1, 1, ORDER, written)
         for copy in (sum_c, sum_y, sum_x):
             copy.wait()
         total[0, 0] += got_c[q].astype(F32)

time: 109 us -> 108 us (level)
  no operation moved by 1% of the time
where the time goes in v6:
time: 108 us
  Pallas kernels  100 us (93%)
  matrix products  3.84 us (4%)
  local copies, waits for them, and re-layouts  2.6 us (2%)
    pallas_call x1, Pallas kernels, local(): pl.pallas_call(functools.partial(filter_kernel, size_x, size_y, node_tota...  100 us
    dot_general x1, matrix products, dot_nt(): lax.dot_general(a, b, (((1,), (1,)), ((), ())), preferred_element_type=F32)  3.84 us
    unnamed x4, local copies, waits for them, and re-layouts  2.6 us

profile of v6, /device:TPU:1, one launch (start us, length us, event | category | flops | bytes accessed | tf_op | source)
XLA Modules:
  0.0 107.5 jit_solution(6891760007113746751)
XLA Ops:
  0.6 2.0 %copy.9.coarse = bf16[16,125,128]{2,1,0:T(8,128)(2,1)} copy(bf16[16,125,128]{2,0,1:T(8,128)(2,1)} %param.7) | data formatting | bytes 1024000 | tf_op args[0]
  2.6 100.4 %filter_twice.1 = (bf16[3456,384]{1,0:T(8,128)(2,1)}, bf16[128,384]{1,0:T(8,128)(2,1)}, f32[128,128]{1,0:T(8,128)}) custom-call(f32[2]{0:T(128)} %window.1, s32[16]{0:T(128)} %targets.1, bf16[16,125,128]{2,1,0:T(8,128)(2,1)} %copy.9.coarse, bf16[288,128]{1,0:T(8,128)(2,1)} %constant.7.table_any, f32[12,12,24]{2,1,0:T(8,128)} %mass_any.1, ...), custom_call_target="tpu_custom_call" | custom-call | flops 4932501504 | bytes 10000000 | tf_op jit(solution)/shard_map/filter_twice/pallas_call | solution.py:790
  103.0 0.0 copy-start
  103.1 3.8 %fusion = f32[3456,128]{1,0:T(8,128)} fusion(bf16[3456,384]{1,0:T(8,128)(2,1)} %get-tuple-element.5, bf16[128,384]{1,0:T(8,128)(2,1)} %get-tuple-element.6), kind=kOutput, calls=%fused_computation | convolution fusion | flops 339738624 | bytes 4521984 | tf_op jit(solution)/shard_map/dot_general | solution.py:73
  106.9 0.0 copy-done
  106.9 0.6 copy.11
Async XLA Ops:
  103.0 3.9 %copy-start = (f32[128,128]{1,0:T(8,128)S(1)}, f32[128,128]{1,0:T(8,128)}, u32[]{:S(2)}) copy-start(f32[128,128]{1,0:T(8,128)} %get-tuple-element.11) | copy-start | bytes 196612

commit v7 on v6

--- a/solution.py
+++ b/solution.py
@@ -127,7 +127,7 @@
     node_total,
     window,
     targets,
-    coarse,
+    coarse_any,
     table_any,
     mass_any,
     pot_any,
@@ -149,6 +149,8 @@
     mass_in,
     pot_in,
     cell_matrix,
+    coarse_rows,
+    coarse,
     slots,
     arrived,
     target_in,
@@ -205,6 +207,7 @@
                 (mass_any, mass_in),
                 (pot_any, pot_in),
                 (table_any, table),
+                (coarse_any, coarse_rows),
             ]
         )
     ]
@@ -231,11 +234,16 @@
             found = jnp.where(ranks[r] == slot, r, found)
         return found & (CELLS - 1)
 
-    last = COARSE_ROWS - 16
-    for index in range(3):
-        slots[index, :, last:COARSE_ROWS] = jnp.zeros((CAPACITY, 16, STATES), BF16)
-    arrived[0:CAPACITY, last:COARSE_ROWS] = jnp.zeros((CAPACITY, 16, STATES), BF16)
-    coarse_count = coarse.shape[1]
+    fetches[4].wait()
+    coarse_count = coarse_rows.shape[0]
+    coarse[:, COARSE_ROWS - 16 :] = jnp.zeros((CELLS, 16, STATES), BF16)
+    for half in range(2):
+        group = slice(half * SLOT, (half + 1) * SLOT)
+        turned = jnp.swapaxes(coarse_rows[...].astype(F32)[:, group], 0, 1)
+        coarse[group, 0:coarse_count] = turned.astype(BF16)
+    for index in (3, 2, 1):
+        for k in range(CAPACITY):
+            slots[index - 1, k] = coarse[record_of(index * CAPACITY + k)]
     tile_lane = lax.broadcasted_iota(jnp.int32, (SLOT, STATES), 1)
     tile = jnp.zeros((SLOT, STATES), jnp.int32)
     for r in range(CELLS):
@@ -254,8 +262,6 @@
         )
         target_copies[index].start()
     for index in (3, 2, 1):
-        for k in range(CAPACITY):
-            slots[index - 1, k, 0:coarse_count] = coarse[record_of(index * CAPACITY + k)]
         record_copies[index] = pltpu.make_async_remote_copy(
             src_ref=slots.at[index - 1],
             dst_ref=arrived.at[pl.ds(index * CAPACITY, CAPACITY)],
@@ -266,9 +272,9 @@
         )
         record_copies[index].start()
     for k in range(CAPACITY):
-        arrived[k, 0:coarse_count] = coarse[record_of(k)]
-
-    for fetch in fetches:
+        arrived[k] = coarse[record_of(k)]
+
+    for fetch in fetches[0:4]:
         fetch.wait()
     place_nodes(mass_in, pot_in, mass, pot)
     spread_matrix(cell_matrix, matrix, from_x, from_y, from_xy)
@@ -786,6 +792,7 @@
     line = (COLUMN, STATES)
     share = STATES // size_y
     messages = 2 * size_y + size_x - 3
+    by_row = coarse_states.transpose(1, 0, 2)
     vmem = pl.BlockSpec(memory_space=pltpu.VMEM)
     filtered, inverse, gram_matrix = pl.pallas_call(
         functools.partial(filter_kernel, size_x, size_y, node_total),
@@ -795,8 +802,7 @@
             jax.ShapeDtypeStruct((STATES, STATES), F32),
         ),
         in_specs=[pl.BlockSpec(memory_space=pltpu.SMEM)] * 2
-        + [vmem]
-        + [pl.BlockSpec(memory_space=pl.ANY)] * 4,
+        + [pl.BlockSpec(memory_space=pl.ANY)] * 5,
         out_specs=(pl.BlockSpec(memory_space=pl.ANY), vmem, vmem),
         scratch_shapes=[
             pltpu.VMEM(padded, F32),
@@ -813,6 +819,8 @@
             pltpu.VMEM(mass_scale.shape, F32),
             pltpu.VMEM(potential.shape, F32),
             pltpu.VMEM(cell_matrix.shape, BF16),
+            pltpu.VMEM(by_row.shape, BF16),
+            pltpu.VMEM((CELLS, COARSE_ROWS, STATES), BF16),
             pltpu.VMEM((3, CAPACITY, COARSE_ROWS, STATES), BF16),
             pltpu.VMEM((4 * CAPACITY, COARSE_ROWS, STATES), BF16),
             pltpu.VMEM((3, SLOT, STATES), jnp.int32),
@@ -844,7 +852,7 @@
             pltpu.SemaphoreType.DMA((3,)),
             pltpu.SemaphoreType.DMA((3,)),
             pltpu.SemaphoreType.DMA,
-            pltpu.SemaphoreType.DMA((4,)),
+            pltpu.SemaphoreType.DMA((5,)),
             pltpu.SemaphoreType.DMA((2, 8)),
             pltpu.SemaphoreType.DMA((2, 8)),
             pltpu.SemaphoreType.DMA((2, messages)),
@@ -860,7 +868,7 @@
     )(
         filter_window,
         record_target,
-        coarse_states,
+        by_row,
         padded_table(),
         mass_scale,
         potential,

time: 108 us -> 106 us (0.981)
  local copies, waits for them, and re-layouts: 2.6 us -> 0.63 us
    unnamed x4 -> x3, local copies, waits for them, and re-layouts: 2.6 us -> 0.63 us
where the time goes in v7:
time: 106 us
  Pallas kernels  100 us (94%)
  matrix products  3.85 us (4%)
    pallas_call x1, Pallas kernels, local(): pl.pallas_call(functools.partial(filter_kernel, size_x, size_y, node_tota...  100 us
    dot_general x1, matrix products, dot_nt(): lax.dot_general(a, b, (((1,), (1,)), ((), ())), preferred_element_type=F32)  3.85 us

profile of v7, /device:TPU:1, one launch (start us, length us, event | category | flops | bytes accessed | tf_op | source)
XLA Modules:
  0.0 105.6 jit_solution(9663786525405049314)
XLA Ops:
  0.6 100.5 %filter_twice.1 = (bf16[3456,384]{1,0:T(8,128)(2,1)}, bf16[128,384]{1,0:T(8,128)(2,1)}, f32[128,128]{1,0:T(8,128)}) custom-call(f32[2]{0:T(128)} %window.1, s32[16]{0:T(128)} %targets.1, bf16[125,16,128]{2,1,0:T(8,128)(2,1)} %bitcast.5, bf16[288,128]{1,0:T(8,128)(2,1)} %constant.7.table_any, f32[12,12,24]{2,1,0:T(8,128)} %mass_any.1, f32[12,12,24]{2,1,0:T(8,128)} %pot_any.1, ...), custom_call_target="tpu_custom_call" | custom-call | flops 4932501504 | bytes 10000000 | tf_op jit(solution)/shard_map/filter_twice/pallas_call | solution.py:797
  101.1 0.0 copy-start
  101.1 3.8 %fusion = f32[3456,128]{1,0:T(8,128)} fusion(bf16[3456,384]{1,0:T(8,128)(2,1)} %get-tuple-element.5, bf16[128,384]{1,0:T(8,128)(2,1)} %get-tuple-element.6), kind=kOutput, calls=%fused_computation | convolution fusion | flops 339738624 | bytes 4521984 | tf_op jit(solution)/shard_map/dot_general | solution.py:73
  105.0 0.0 copy-done
  105.0 0.6 copy.10
Async XLA Ops:
  101.1 3.9 %copy-start = (f32[128,128]{1,0:T(8,128)S(1)}, f32[128,128]{1,0:T(8,128)}, u32[]{:S(2)}) copy-start(f32[128,128]{1,0:T(8,128)} %get-tuple-element.11) | copy-start | bytes 196612

commit v8 on v7

--- a/solution.py
+++ b/solution.py
@@ -428,6 +428,12 @@
         result = mass[index] * full + (pot[index] - center) * value
         block[(1 - q,) + index] = alpha * result - beta * block[(1 - q,) + index]
 
+    width = COUNT_Z * STATES
+
+    def gather_ahead(q):
+        gather(q, 1, 0, rhs_two, 0)
+        gather(q, 1, 1, rhs_two, width)
+
     def one_apply(t):
         q = t % 2
         first = (t % CHEB_DEGREE) == 0
@@ -451,10 +457,7 @@
         for copy in values[0:3]:
             copy.start()
         written = set()
-        width = COUNT_Z * STATES
         inner = FACE * ORDER
-        gather(q, 1, 0, rhs_two, 0)
-        gather(q, 1, 1, rhs_two, width)
         face = dot_nn(matrix[inner : inner + FACE, 0:inner], rhs_two[...])
 
         def face_line(f, b):
@@ -531,15 +534,17 @@
             taken_rows(0, behind_y + [along_y[0]] + none, h)
         product = dot_nn(from_y[0:FACE, FACE : 2 * FACE], rhs_taken[0:FACE, :])
         add_product(product, 0, 1, 1, ORDER, written)
-        for copy in (sum_c, sum_y, sum_x):
+        sum_y.wait()
+        for x, line in enumerate(widen([got_y[q, i] for i in range(LINES)], grow_own)):
+            total[x, 0] += line
+        finish(q, (slice(1, ROWS), 0), alpha, beta)
+        gather_ahead(1 - q)
+        for copy in (sum_c, sum_x):
             copy.wait()
         total[0, 0] += got_c[q].astype(F32)
-        for x, line in enumerate(widen([got_y[q, i] for i in range(LINES)], grow_own)):
-            total[x, 0] += line
         for y, line in enumerate(widen([got_x[q, i] for i in range(LINES)], grow_own)):
             total[0, y] += line
         finish(q, (0, slice(0, ROWS)), alpha, beta)
-        finish(q, (slice(1, ROWS), 0), alpha, beta)
 
     share = STATES // size_y
 
@@ -647,9 +652,11 @@
                 return inner
 
             lax.fori_loop(0, ROWS, turn, 0)
+            gather_ahead((CHEB_DEGREE + 2) % 2)
 
         return carry
 
+    gather_ahead(0)
     lax.fori_loop(0, 2 * CHEB_DEGREE, step, 0)
     begin_sum(1, 0)
     store = pltpu.make_async_copy(split, filtered_out, store_sem)

time: 106 us -> 107 us (level)
  Pallas kernels: 100 us -> 102 us
    pallas_call x1, Pallas kernels: 100 us -> 102 us  [local(): pl.pallas_call(functools.partial(filter_kernel, size_x, size_y, node_tota...]
where the time goes in v8:
time: 107 us
  Pallas kernels  102 us (95%)
  matrix products  3.85 us (4%)
    pallas_call x1, Pallas kernels, local(): pl.pallas_call(functools.partial(filter_kernel, size_x, size_y, node_tota...  102 us
    dot_general x1, matrix products, dot_nt(): lax.dot_general(a, b, (((1,), (1,)), ((), ())), preferred_element_type=F32)  3.85 us

profile of v8, /device:TPU:1, one launch (start us, length us, event | category | flops | bytes accessed | tf_op | source)
XLA Modules:
  0.0 107.3 jit_solution(17599095528160617782)
XLA Ops:
  0.6 102.2 %filter_twice.1 = (bf16[3456,384]{1,0:T(8,128)(2,1)}, bf16[128,384]{1,0:T(8,128)(2,1)}, f32[128,128]{1,0:T(8,128)}) custom-call(f32[2]{0:T(128)} %window.1, s32[16]{0:T(128)} %targets.1, bf16[125,16,128]{2,1,0:T(8,128)(2,1)} %bitcast.5, bf16[288,128]{1,0:T(8,128)(2,1)} %constant.7.table_any, f32[12,12,24]{2,1,0:T(8,128)} %mass_any.1, f32[12,12,24]{2,1,0:T(8,128)} %pot_any.1, ...), custom_call_target="tpu_custom_call" | custom-call | flops 4932501504 | bytes 10000000 | tf_op jit(solution)/shard_map/filter_twice/pallas_call | solution.py:804
  102.8 0.0 copy-start
  102.8 3.8 %fusion = f32[3456,128]{1,0:T(8,128)} fusion(bf16[3456,384]{1,0:T(8,128)(2,1)} %get-tuple-element.5, bf16[128,384]{1,0:T(8,128)(2,1)} %get-tuple-element.6), kind=kOutput, calls=%fused_computation | convolution fusion | flops 339738624 | bytes 4521984 | tf_op jit(solution)/shard_map/dot_general | solution.py:73
  106.6 0.0 copy-done
  106.6 0.6 copy.10
Async XLA Ops:
  102.8 3.9 %copy-start = (f32[128,128]{1,0:T(8,128)S(1)}, f32[128,128]{1,0:T(8,128)}, u32[]{:S(2)}) copy-start(f32[128,128]{1,0:T(8,128)} %get-tuple-element.11) | copy-start | bytes 196612

commit v9 on v7

--- a/solution.py
+++ b/solution.py
@@ -531,15 +531,16 @@
             taken_rows(0, behind_y + [along_y[0]] + none, h)
         product = dot_nn(from_y[0:FACE, FACE : 2 * FACE], rhs_taken[0:FACE, :])
         add_product(product, 0, 1, 1, ORDER, written)
-        for copy in (sum_c, sum_y, sum_x):
+        sum_y.wait()
+        for x, line in enumerate(widen([got_y[q, i] for i in range(LINES)], grow_own)):
+            total[x, 0] += line
+        finish(q, (slice(1, ROWS), 0), alpha, beta)
+        for copy in (sum_c, sum_x):
             copy.wait()
         total[0, 0] += got_c[q].astype(F32)
-        for x, line in enumerate(widen([got_y[q, i] for i in range(LINES)], grow_own)):
-            total[x, 0] += line
         for y, line in enumerate(widen([got_x[q, i] for i in range(LINES)], grow_own)):
             total[0, y] += line
         finish(q, (0, slice(0, ROWS)), alpha, beta)
-        finish(q, (slice(1, ROWS), 0), alpha, beta)
 
     share = STATES // size_y
 

time: 106 us -> 106 us (level)
  no operation moved by 1% of the time
where the time goes in v9:
time: 106 us
  Pallas kernels  101 us (95%)
  matrix products  3.85 us (4%)
    pallas_call x1, Pallas kernels, local(): pl.pallas_call(functools.partial(filter_kernel, size_x, size_y, node_tota...  101 us
    dot_general x1, matrix products, dot_nt(): lax.dot_general(a, b, (((1,), (1,)), ((), ())), preferred_element_type=F32)  3.85 us

profile of v9, /device:TPU:1, one launch (start us, length us, event | category | flops | bytes accessed | tf_op | source)
XLA Modules:
  0.0 106.3 jit_solution(6973212270650056645)
XLA Ops:
  0.6 101.2 %filter_twice.1 = (bf16[3456,384]{1,0:T(8,128)(2,1)}, bf16[128,384]{1,0:T(8,128)(2,1)}, f32[128,128]{1,0:T(8,128)}) custom-call(f32[2]{0:T(128)} %window.1, s32[16]{0:T(128)} %targets.1, bf16[125,16,128]{2,1,0:T(8,128)(2,1)} %bitcast.5, bf16[288,128]{1,0:T(8,128)(2,1)} %constant.7.table_any, f32[12,12,24]{2,1,0:T(8,128)} %mass_any.1, f32[12,12,24]{2,1,0:T(8,128)} %pot_any.1, ...), custom_call_target="tpu_custom_call" | custom-call | flops 4932501504 | bytes 10000000 | tf_op jit(solution)/shard_map/filter_twice/pallas_call | solution.py:798
  101.8 0.0 copy-start
  101.8 3.8 %fusion = f32[3456,128]{1,0:T(8,128)} fusion(bf16[3456,384]{1,0:T(8,128)(2,1)} %get-tuple-element.5, bf16[128,384]{1,0:T(8,128)(2,1)} %get-tuple-element.6), kind=kOutput, calls=%fused_computation | convolution fusion | flops 339738624 | bytes 4521984 | tf_op jit(solution)/shard_map/dot_general | solution.py:73
  105.7 0.0 copy-done
  105.7 0.6 copy.10
Async XLA Ops:
  101.8 3.9 %copy-start = (f32[128,128]{1,0:T(8,128)S(1)}, f32[128,128]{1,0:T(8,128)}, u32[]{:S(2)}) copy-start(f32[128,128]{1,0:T(8,128)} %get-tuple-element.11) | copy-start | bytes 196612
